TPU v7x, 32 devices: a whole 2x2x4 slice. The times are simulated.
32 devices in a mesh: dp: 16 (over z, x, core), rep: 2 (over y).
Axes of the slice: x: 2, y: 2, z: 4, core: 2. Of those that a mesh axis runs over, the one named last changes fastest.
Arguments:
- tokens: bfloat16 [49152, 768], P(('dp', 'rep')), may hold values from -12 to 12
- cotangent: bfloat16 [49152, 768], P(('dp', 'rep')), may hold values from -6 to 6
- lengths: int32 [96, 3], P(('dp', 'rep')), may hold values from 1 to 256, 512 in all within a row
- qkv_weight: float32 [768, 2304], P('dp'), may hold values from -0.21875 to 0.21875
- attn_out_weight: float32 [768, 768], P('dp'), may hold values from -1.75 to 1.75
- mlp_in_weight: float32 [768, 2304], P('dp'), may hold values from -0.21875 to 0.21875
- mlp_out_weight: float32 [1152, 768], P('dp'), may hold values from -0.1875 to 0.1875
- norm_gains: float32 [768, 2], P('dp'), may hold values from 0.5 to 1.5
- qkv_first: float32 [768, 2304], P('dp'), may hold values from -160 to 160
- qkv_second: float32 [768, 2304], P('dp'), may hold values from 1003.094 to 4012.4253
- attn_first: float32 [768, 768], P('dp'), may hold values from -20 to 20
- attn_second: float32 [768, 768], P('dp'), may hold values from 15.67359 to 62.693375
- mlp_in_first: float32 [768, 2304], P('dp'), may hold values from -80 to 80
- mlp_in_second: float32 [768, 2304], P('dp'), may hold values from 334.3663 to 1337.4751
- mlp_out_first: float32 [1152, 768], P('dp'), may hold values from -112 to 112
- mlp_out_second: float32 [1152, 768], P('dp'), may hold values from 501.547 to 2006.188
- gains_first: float32 [768, 2], P('dp'), may hold values from -160 to 160
- gains_second: float32 [768, 2], P('dp'), may hold values from 1003.094 to 4012.4253
Outputs:
- activations: bfloat16 [49152, 768], P(('dp', 'rep'))
- input_grad: float32 [49152, 768], P(('dp', 'rep'))
- qkv_new: float32 [768, 2304], P('dp')
- qkv_first_new: float32 [768, 2304], P('dp')
- qkv_second_new: float32 [768, 2304], P('dp')
- attn_out_new: float32 [768, 768], P('dp')
- attn_first_new: float32 [768, 768], P('dp')
- attn_second_new: float32 [768, 768], P('dp')
- mlp_in_new: float32 [768, 2304], P('dp')
- mlp_in_first_new: float32 [768, 2304], P('dp')
- mlp_in_second_new: float32 [768, 2304], P('dp')
- mlp_out_new: float32 [1152, 768], P('dp')
- mlp_out_first_new: float32 [1152, 768], P('dp')
- mlp_out_second_new: float32 [1152, 768], P('dp')
- gains_new: float32 [768, 2], P('dp')
- gains_first_new: float32 [768, 2], P('dp')
- gains_second_new: float32 [768, 2], P('dp')
Inputs may be any that keep to these rules, and one draw needn't show every extreme that they name: Row m holds in order the lengths of the 3 sequences packed into micro-batch m; every row sums to 512.
All inputs are finite; a program needn't handle non-finite values.
Results may differ from a plain program's by a relative error of at most 0.014.
The roundings to bfloat16 on the way count: a program that leaves them out, or rounds other values in their place, can miss the bound.
Values may be sent and summed in bfloat16 or wider, within the bound.
A program may use at most 256 MiB of HBM per device.

v0:
```python
import math

import jax
import jax.numpy as jnp
from jax import lax
from jax.sharding import PartitionSpec as P

HEADS = 12
HEAD_DIM = 64
STEP = 10


beta_one = 0.9
beta_two = 0.98
adam_eps = 1e-06
decay_rate = 1e-05
inv_root_two = 0.7071067811865476
inv_root_tau = 0.3989422804014327


def normalize(values):
    centred = values - jnp.mean(values, -1, keepdims=True)
    inv_std = lax.rsqrt(jnp.mean(centred * centred, -1, keepdims=True) + 1e-05)
    return (centred * inv_std, inv_std)


def norm_back(grad_out, x_hat, inv_std, gain_col):
    scaled = grad_out * gain_col
    return inv_std * (
        scaled
        - jnp.mean(scaled, -1, keepdims=True)
        - x_hat * jnp.mean(scaled * x_hat, -1, keepdims=True)
    )


def rotate_half(values):
    half_dim = values.shape[-1] // 2
    return jnp.concatenate([-values[..., half_dim:], values[..., :half_dim]], -1)


def rope_tables(positions):
    freq_idx = jnp.arange(HEAD_DIM // 2).astype(jnp.float32)
    inv_freq = jnp.exp(freq_idx * (-2.0 * math.log(160000.0) / HEAD_DIM))
    angles = positions.astype(jnp.float32)[:, None] * inv_freq[None, :]
    angles = jnp.concatenate([angles, angles], -1)[:, None, :]
    return (jnp.cos(angles), jnp.sin(angles))


def segments(seq_lens, row_count):
    ends = jnp.cumsum(seq_lens)
    row_idx = jnp.arange(row_count)
    seg_ids = jnp.sum((row_idx[:, None] >= ends[None, :]).astype(jnp.int32), 1)
    starts = ends - seq_lens
    pick = seg_ids[:, None] == jnp.arange(seq_lens.shape[0])[None, :]
    positions = row_idx - jnp.sum(jnp.where(pick, starts[None, :], 0), 1)
    return (seg_ids, positions)


def contract_rows(left, right):
    return lax.dot_general(
        left, right, (((0,), (0,)), ((), ())), preferred_element_type=jnp.float32
    )


def contract_cols(left, right):
    return lax.dot_general(
        left, right, (((1,), (1,)), ((), ())), preferred_element_type=jnp.float32
    )


def forward_pass(x_rows, seg_ids, positions, weights):
    w_qkv, w_attn, w_in, w_out, gains_low = weights
    gain_vals = gains_low.astype(jnp.float32)
    row_count, width = x_rows.shape
    head_size = width // HEADS
    x_float = x_rows.astype(jnp.float32)
    hat_one, inv_one = normalize(x_float)
    h_one = (hat_one * gain_vals[:, 0]).astype(jnp.bfloat16)
    qkv_all = jnp.dot(h_one, w_qkv, preferred_element_type=jnp.float32)
    q_part = qkv_all[:, :width].reshape(row_count, HEADS, head_size)
    k_part = qkv_all[:, width : 2 * width].reshape(row_count, HEADS, head_size)
    v_part = qkv_all[:, 2 * width :].reshape(row_count, HEADS, head_size)
    cos_tab, sin_tab = rope_tables(positions)
    q_rot = (q_part * cos_tab + rotate_half(q_part) * sin_tab).astype(jnp.bfloat16)
    k_rot = (k_part * cos_tab + rotate_half(k_part) * sin_tab).astype(jnp.bfloat16)
    v_low = v_part.astype(jnp.bfloat16)
    same_seg = (seg_ids[:, None] == seg_ids[None, :])[None]
    scores = jnp.einsum("qhd,khd->hqk", q_rot, k_rot, preferred_element_type=jnp.float32) * 0.125
    scores = jnp.where(same_seg, scores, -1e30)
    top_score = jnp.max(scores, -1, keepdims=True)
    expo = jnp.exp(scores - top_score)
    total = jnp.sum(expo, -1, keepdims=True)
    probs = (expo / total).astype(jnp.bfloat16)
    contexts = jnp.einsum("hqk,khd->qhd", probs, v_low, preferred_element_type=jnp.float32)
    totals = top_score + jnp.log(total)
    context = contexts.reshape(row_count, width).astype(jnp.bfloat16)
    middle = x_float + jnp.dot(context, w_attn, preferred_element_type=jnp.float32)
    hat_two, inv_two = normalize(middle)
    h_two = (hat_two * gain_vals[:, 1]).astype(jnp.bfloat16)
    gate_up = jnp.dot(h_two, w_in, preferred_element_type=jnp.float32)
    ff_width = w_out.shape[0]
    act_in = gate_up[:, :ff_width]
    gate_in = gate_up[:, ff_width:]
    cdf_vals = 0.5 * (1.0 + lax.erf(act_in * inv_root_two))
    act_out = act_in * cdf_vals
    hidden = (act_out * gate_in).astype(jnp.bfloat16)
    result = (middle + jnp.dot(hidden, w_out, preferred_element_type=jnp.float32)).astype(
        jnp.bfloat16
    )
    saved = (
        hat_one,
        inv_one,
        h_one,
        q_rot,
        k_rot,
        v_low,
        same_seg,
        totals,
        cos_tab,
        sin_tab,
        context,
        hat_two,
        inv_two,
        h_two,
        act_in,
        gate_in,
        cdf_vals,
        act_out,
        hidden,
    )
    return (result, saved)


def backward_pass(saved, grad_rows, weights):
    (
        hat_one,
        inv_one,
        h_one,
        q_rot,
        k_rot,
        v_low,
        same_seg,
        log_total,
        cos_tab,
        sin_tab,
        context,
        hat_two,
        inv_two,
        h_two,
        act_in,
        gate_in,
        cdf_vals,
        act_out,
        hidden,
    ) = saved
    w_qkv, w_attn, w_in, w_out, gains_low = weights
    gain_vals = gains_low.astype(jnp.float32)
    row_count, width = grad_rows.shape
    head_size = width // HEADS
    grad_float = grad_rows.astype(jnp.float32)
    grad_hidden = contract_cols(grad_rows, w_out)
    grad_wo = contract_rows(hidden, grad_rows)
    grad_act = (
        grad_hidden * gate_in * (cdf_vals + act_in * inv_root_tau * jnp.exp(-0.5 * act_in * act_in))
    )
    grad_gate = grad_hidden * act_out
    grad_gu = jnp.concatenate([grad_act, grad_gate], 1).astype(jnp.bfloat16)
    grad_wi = contract_rows(h_two, grad_gu)
    grad_h_two = contract_cols(grad_gu, w_in)
    grad_mid = grad_float + norm_back(grad_h_two, hat_two, inv_two, gain_vals[:, 1])
    grad_g_two = jnp.sum(grad_h_two * hat_two, 0)
    grad_mid_low = grad_mid.astype(jnp.bfloat16)
    grad_wa = contract_rows(context, grad_mid_low)
    grad_ctx = (
        contract_cols(grad_mid_low, w_attn)
        .astype(jnp.bfloat16)
        .reshape(row_count, HEADS, head_size)
    )
    scores = jnp.einsum("qhd,khd->hqk", q_rot, k_rot, preferred_element_type=jnp.float32) * 0.125
    scores = jnp.where(same_seg, scores, -1e30)
    probs = jnp.exp(scores - log_total)
    probs_low = probs.astype(jnp.bfloat16)
    grad_probs = jnp.einsum("qhd,khd->hqk", grad_ctx, v_low, preferred_element_type=jnp.float32)
    row_dots = jnp.sum(probs * grad_probs, -1, keepdims=True)
    grad_scores = (probs * (grad_probs - row_dots)).astype(jnp.bfloat16)
    grad_q_parts = (
        jnp.einsum("hqk,khd->qhd", grad_scores, k_rot, preferred_element_type=jnp.float32) * 0.125
    )
    grad_k = (
        jnp.einsum("hqk,qhd->khd", grad_scores, q_rot, preferred_element_type=jnp.float32) * 0.125
    )
    grad_v = jnp.einsum("hqk,qhd->khd", probs_low, grad_ctx, preferred_element_type=jnp.float32)
    grad_q_pre = grad_q_parts * cos_tab - rotate_half(grad_q_parts * sin_tab)
    grad_k_pre = grad_k * cos_tab - rotate_half(grad_k * sin_tab)
    grad_qkv = jnp.concatenate(
        [
            grad_q_pre.reshape(row_count, width),
            grad_k_pre.reshape(row_count, width),
            grad_v.reshape(row_count, width),
        ],
        1,
    ).astype(jnp.bfloat16)
    grad_wq = contract_rows(h_one, grad_qkv)
    grad_h_one = contract_cols(grad_qkv, w_qkv)
    grad_x = grad_mid + norm_back(grad_h_one, hat_one, inv_one, gain_vals[:, 0])
    grad_g_one = jnp.sum(grad_h_one * hat_one, 0)
    grad_gains = jnp.stack([grad_g_one, grad_g_two], 1)
    return (grad_x, (grad_wq, grad_wa, grad_wi, grad_wo, grad_gains))


def adam_update(weight, first, second, grad, rate):
    first_new = beta_one * first + (1.0 - beta_one) * grad
    second_new = beta_two * second + (1.0 - beta_two) * grad * grad
    corr_one = 1.0 - beta_one**STEP
    corr_two = 1.0 - beta_two**STEP
    direction = first_new / corr_one / (jnp.sqrt(second_new / corr_two) + adam_eps)
    return (weight - rate * (direction + decay_rate * weight), first_new, second_new)


def local(
    tokens,
    cotangent,
    lengths,
    qkv_weight,
    attn_out_weight,
    mlp_in_weight,
    mlp_out_weight,
    norm_gains,
    qkv_first,
    qkv_second,
    attn_first,
    attn_second,
    mlp_in_first,
    mlp_in_second,
    mlp_out_first,
    mlp_out_second,
    gains_first,
    gains_second,
):
    low_qkv = qkv_weight.astype(jnp.bfloat16)
    low_attn = attn_out_weight.astype(jnp.bfloat16)
    low_in = mlp_in_weight.astype(jnp.bfloat16)
    low_out = mlp_out_weight.astype(jnp.bfloat16)
    low_gains = norm_gains.astype(jnp.bfloat16)
    micro_count = lengths.shape[0]
    row_count = tokens.shape[0] // micro_count
    width = tokens.shape[1]
    ff_width = mlp_in_weight.shape[1] // 2
    acc_q = jnp.zeros((width, 3 * width), jnp.float32)
    acc_a = jnp.zeros((width, width), jnp.float32)
    acc_i = jnp.zeros((width, 2 * ff_width), jnp.float32)
    acc_o = jnp.zeros((ff_width, width), jnp.float32)
    acc_g = jnp.zeros((width, 2), jnp.float32)
    result_parts = []
    grad_parts = []
    for part_no in range(micro_count):
        x_rows = tokens[part_no * row_count : (part_no + 1) * row_count]
        grad_rows = cotangent[part_no * row_count : (part_no + 1) * row_count]
        seg_ids, positions = segments(lengths[part_no], row_count)
        fwd_full = (
            lax.all_gather(low_qkv, "dp", axis=0, tiled=True),
            lax.all_gather(low_attn, "dp", axis=0, tiled=True),
            lax.all_gather(low_in, "dp", axis=0, tiled=True),
            lax.all_gather(low_out, "dp", axis=0, tiled=True),
            lax.all_gather(low_gains, "dp", axis=0, tiled=True),
        )
        result, saved = forward_pass(x_rows, seg_ids, positions, fwd_full)
        bwd_full = (
            lax.all_gather(low_qkv, "dp", axis=0, tiled=True),
            lax.all_gather(low_attn, "dp", axis=0, tiled=True),
            lax.all_gather(low_in, "dp", axis=0, tiled=True),
            lax.all_gather(low_out, "dp", axis=0, tiled=True),
            lax.all_gather(low_gains, "dp", axis=0, tiled=True),
        )
        grad_x, terms = backward_pass(saved, grad_rows, bwd_full)
        result_parts.append(result)
        grad_parts.append(grad_x)
        acc_q = acc_q + terms[0]
        acc_a = acc_a + terms[1]
        acc_i = acc_i + terms[2]
        acc_o = acc_o + terms[3]
        acc_g = acc_g + terms[4]
    summed = lax.psum((acc_q, acc_a, acc_i, acc_o, acc_g), "rep")
    owned_sums = (
        lax.psum_scatter(summed[0], "dp", scatter_dimension=0, tiled=True),
        lax.psum_scatter(summed[1], "dp", scatter_dimension=0, tiled=True),
        lax.psum_scatter(summed[2], "dp", scatter_dimension=0, tiled=True),
        lax.psum_scatter(summed[3], "dp", scatter_dimension=0, tiled=True),
        lax.psum_scatter(summed[4], "dp", scatter_dimension=0, tiled=True),
    )
    qkv_res = adam_update(qkv_weight, qkv_first, qkv_second, owned_sums[0], 0.03)
    attn_res = adam_update(attn_out_weight, attn_first, attn_second, owned_sums[1], 0.3)
    in_res = adam_update(mlp_in_weight, mlp_in_first, mlp_in_second, owned_sums[2], 0.03)
    out_res = adam_update(mlp_out_weight, mlp_out_first, mlp_out_second, owned_sums[3], 0.03)
    gain_res = adam_update(norm_gains, gains_first, gains_second, owned_sums[4], 0.5)
    activations = jnp.concatenate(result_parts, 0)
    input_grad = jnp.concatenate(grad_parts, 0)
    return (
        activations,
        input_grad,
        qkv_res[0],
        qkv_res[1],
        qkv_res[2],
        attn_res[0],
        attn_res[1],
        attn_res[2],
        in_res[0],
        in_res[1],
        in_res[2],
        out_res[0],
        out_res[1],
        out_res[2],
        gain_res[0],
        gain_res[1],
        gain_res[2],
    )


def solution(mesh):
    in_specs = (
        P(("dp", "rep"), None),
        P(("dp", "rep"), None),
        P(("dp", "rep"), None),
        P("dp", None),
        P("dp", None),
        P("dp", None),
        P("dp", None),
        P("dp", None),
        P("dp", None),
        P("dp", None),
        P("dp", None),
        P("dp", None),
        P("dp", None),
        P("dp", None),
        P("dp", None),
        P("dp", None),
        P("dp", None),
        P("dp", None),
    )
    out_specs = (
        P(("dp", "rep"), None),
        P(("dp", "rep"), None),
        P("dp", None),
        P("dp", None),
        P("dp", None),
        P("dp", None),
        P("dp", None),
        P("dp", None),
        P("dp", None),
        P("dp", None),
        P("dp", None),
        P("dp", None),
        P("dp", None),
        P("dp", None),
        P("dp", None),
        P("dp", None),
        P("dp", None),
    )
    return jax.shard_map(local, mesh=mesh, in_specs=in_specs, out_specs=out_specs, check_vma=False)
```

profile of v0, /device:TPU:0, one launch (start us, length us, event | category | flops | bytes accessed | tf_op | source)
XLA Modules:
  0.0 685.1 jit_solution(7851829456084993571)
XLA Ops:
  18.2 23.1 %all-gather = bf16[16,48,2]{1,2,0:T(2,128)(2,1)S(1)} all-gather(bf16[1,48,2]{1,2,0:T(2,128)(2,1)S(1)} %convert_bitcast_fusion), channel_id=1, replica_groups=mesh['dp'=16,'rep'=2] {'dp'}, dimensions={0}, use_global_device_ids=true | all-gather | bytes 3264 | tf_op jit(solution)/shard_map/all_gather | solution.py:265
  43.5 17.3 %all-gather.6.cloned.1.call-done = bf16[768,2304]{1,0:T(8,128)(2,1)} async-done(((bf16[48,2304]{1,0:T(8,128)(2,1)}), bf16[768,2304]{1,0:T(8,128)(2,1)}) %all-gather.6.cloned.1.call-update) | async-done | bytes 3538960 | tf_op jit(solution)/shard_map/all_gather | solution.py:261
  60.9 4.1 fusion.179
  78.5 3.0 copy.154
  90.0 3.1 copy.163
  95.9 3.0 copy.162
  104.1 3.7 fusion.86
  115.1 5.5 fusion.107
  131.1 3.0 copy.158
  138.3 4.1 fusion.82
  149.4 3.8 fusion.108
  160.2 3.7 fusion
  164.8 6.9 %fusion.183 = f32[512,2304]{1,0:T(8,128)} fusion(bf16[768,2304]{1,0:T(8,128)(2,1)} %all-gather.10.cloned.1.call-done, f32[512,768]{1,0:T(8,128)} %copy-done.15, f32[512]{0:T(512)S(1)} %copy-done.145, f32[512]{0:T(512)S(1)} %broadcast_multiply_fusion.21, f32[768]{0:T(1024)S(1)} %get-tuple-element.45), kind=kOutput, calls=%fused_computation.376 | convolution fusion | flops 1813512192 | bytes 9837568 | tf_op jit(solution)/shard_map/dot_general | solution.py:100
  171.7 4.3 fusion.182
  176.0 15.0 %all-gather.12.cloned.1.call-done = bf16[1152,768]{1,0:T(8,128)(2,1)} async-done(((bf16[72,768]{1,0:T(8,128)(2,1)}), bf16[1152,768]{1,0:T(8,128)(2,1)}) %all-gather.12.cloned.1.call-update) | async-done | bytes 1769488 | tf_op jit(solution)/shard_map/all_gather | solution.py:264
  190.9 6.4 fusion.35
  197.4 5.3 fusion.30
  205.5 4.3 multiply_reduce_fusion.4
  212.1 8.4 %fusion.109 = bf16[12,64,512]{2,1,0:T(8,128)(2,1)S(1)} fusion(bf16[512,12,64]{0,2,1:T(8,128)(2,1)} %bitcast.192, f32[12,512]{1,0:T(8,128)S(1)} %fusion, f32[12,512]{1,0:T(8,128)S(1)} %get-tuple-element.162, f32[12,512,512]{1,2,0:T(8,128)} %copy-done.2, pred[512,512]{0,1:T(8,128)(4,1)} %broadcast_compare_fusion.2), kind=kOutput, calls=%fused_computation.206 | convolution fusion | flops 418775040 | bytes 14467072 | tf_op jit(solution)/shard_map/hqk,khd->qhd/dot_general | solution.py:94
  228.3 5.2 multiply_add_fusion.1
  252.9 14.1 %multiply_reduce_fusion.2 = (f32[12,512]{1,0:T(8,128)S(1)}, f32[12,512,512]{1,2,0:T(8,128)}) fusion(f32[12,512]{1,0:T(8,128)S(1)} %log_add_fusion.2, f32[12,512,512]{1,2,0:T(8,128)} %copy-done.2, pred[512,512]{0,1:T(8,128)(4,1)} %broadcast_compare_fusion.2, bf16[512,12,64]{0,2,1:T(8,128)(2,1)} %bitcast.186, bf16[512,12,64]{0,2,1:T(8,128)(2,1)} %bitcast.193), kind=kOutput, calls=%fused_computation.7 | convolution fusion | flops 418375680 | bytes 27049984 | tf_op jit(solution)/shard_map/qhd,khd->hqk/dot_general | solution.py:183
  267.0 7.5 %multiply_convert_fusion.2 = bf16[12,512,512]{1,2,0:T(8,128)(2,1)S(1)} fusion(f32[12,512,512]{1,2,0:T(8,128)} %get-tuple-element.169, f32[12,512]{1,0:T(8,128)S(1)} %get-tuple-element.168, f32[12,512]{1,0:T(8,128)S(1)} %log_add_fusion.2, f32[12,512,512]{1,2,0:T(8,128)S(1)} %bitcast.169, pred[512,512]{0,1:T(8,128)(4,1)S(1)} %copy-done.34), kind=kLoop, calls=%fused_computation.6 | loop fusion | flops 18874368 | bytes 31768576 | tf_op jit(solution)/shard_map/convert_element_type | solution.py:185
  277.7 3.3 bitcast_multiply_fusion.10
  281.1 3.6 convolution_convert_fusion.1
  295.5 6.9 %fusion.94 = f32[768,2304]{1,0:T(8,128)} fusion(bf16[512,1152]{1,0:T(8,128)(2,1)} %copy-done.84, bf16[512,1152]{1,0:T(8,128)(2,1)} %copy-done.83, f32[512,768]{1,0:T(8,128)S(1)} %copy-done.42, f32[512]{0:T(512)S(1)} %copy-done.142, f32[512]{0:T(512)S(1)} %broadcast_multiply_fusion.23, f32[768]{0:T(1024)S(1)} %get-tuple-element.45), kind=kOutput, calls=%fused_computation.191 | convolution fusion | flops 1818230784 | bytes 11017216 | tf_op jit(solution)/shard_map/dot_general | solution.py:60
  302.4 5.1 fusion.96
  307.5 6.9 %multiply_reduce_fusion.1 = (f32[12,512]{1,0:T(8,128)S(1)}, f32[12,512,512]{1,2,0:T(8,128)}) fusion(f32[12,512]{1,0:T(8,128)S(1)} %log_add_fusion.1, f32[12,512,512]{1,2,0:T(8,128)S(1)} %bitcast.167, pred[512,512]{0,1:T(8,128)(4,1)S(1)} %broadcast_compare_fusion.1, bf16[512,12,64]{0,2,1:T(8,128)(2,1)S(1)} %bitcast.190, bf16[512,12,64]{0,2,1:T(8,128)(2,1)S(1)} %bitcast.185), kind=kOutput, calls=%fused_computation.4 | convolution fusion | flops 418375680 | bytes 27049984 | tf_op jit(solution)/shard_map/qhd,khd->hqk/dot_general | solution.py:183
  314.4 7.3 %multiply_convert_fusion.1 = bf16[12,512,512]{1,2,0:T(8,128)(2,1)S(1)} fusion(f32[12,512,512]{1,2,0:T(8,128)} %get-tuple-element.175, f32[12,512]{1,0:T(8,128)S(1)} %get-tuple-element.174, f32[12,512]{1,0:T(8,128)S(1)} %log_add_fusion.1, f32[12,512,512]{1,2,0:T(8,128)S(1)} %bitcast.167, pred[512,512]{0,1:T(8,128)(4,1)S(1)} %broadcast_compare_fusion.1), kind=kLoop, calls=%fused_computation.3 | loop fusion | flops 18874368 | bytes 31768576 | tf_op jit(solution)/shard_map/convert_element_type | solution.py:185
  321.7 3.1 fusion.196
  328.3 9.2 %add_add_fusion = f32[768,2304]{1,0:T(8,128)} fusion(f32[768,2304]{1,0:T(8,128)S(1)} %copy-done.4, f32[768,2304]{1,0:T(8,128)} %fusion.94, bf16[512,1152]{1,0:T(8,128)(2,1)} %copy-done.82, bf16[512,1152]{1,0:T(8,128)(2,1)} %copy-done.81, f32[512,768]{1,0:T(8,128)S(1)} %copy-done.18, f32[512]{0:T(512)S(1)} %copy-done.146, f32[512]{0:T(512)S(1)} %copy-done.139, ...), kind=kOutput, calls=%fused_computation.24 | convolution fusion | flops 1821769728 | bytes 25172992 | tf_op jit(solution)/shard_map/dot_general | solution.py:60
  338.6 6.1 bitcast_multiply_fusion.6
  348.1 11.0 %multiply_reduce_fusion = (f32[12,512]{1,0:T(8,128)S(1)}, f32[12,512,512]{1,2,0:T(8,128)}) fusion(f32[12,512]{1,0:T(8,128)S(1)} %copy-done.120, f32[12,512,512]{1,2,0:T(8,128)} %copy-done, pred[512,512]{0,1:T(8,128)(4,1)S(1)} %copy-done.32, bf16[512,12,64]{0,2,1:T(8,128)(2,1)S(1)} %bitcast.188, bf16[512,12,64]{0,2,1:T(8,128)(2,1)S(1)} %bitcast.183), kind=kOutput, calls=%fused_computation.1 | convolution fusion | flops 418375680 | bytes 27049984 | tf_op jit(solution)/shard_map/qhd,khd->hqk/dot_general | solution.py:183
  359.2 7.1 %multiply_convert_fusion = bf16[12,512,512]{1,2,0:T(8,128)(2,1)S(1)} fusion(f32[12,512,512]{1,2,0:T(8,128)} %get-tuple-element.172, f32[12,512]{1,0:T(8,128)S(1)} %get-tuple-element.171, f32[12,512]{1,0:T(8,128)S(1)} %copy-done.120, f32[12,512,512]{1,2,0:T(8,128)S(1)} %bitcast.165, pred[512,512]{0,1:T(8,128)(4,1)S(1)} %copy-done.32), kind=kLoop, calls=%fused_computation | loop fusion | flops 18874368 | bytes 31768576 | tf_op jit(solution)/shard_map/convert_element_type | solution.py:185
  380.6 7.4 %fusion.101 = bf16[12,64,512]{2,1,0:T(8,128)(2,1)} fusion(bf16[512,12,64]{0,2,1:T(8,128)(2,1)S(1)} %bitcast.191, f32[12,512]{1,0:T(8,128)S(1)} %copy-done.119, f32[12,512,512]{1,2,0:T(8,128)} %copy-done.1, pred[512,512]{0,1:T(8,128)(4,1)S(1)} %broadcast_compare_fusion.1), kind=kOutput, calls=%fused_computation.202 | convolution fusion | flops 415629312 | bytes 14442496 | tf_op jit(solution)/shard_map/hqk,qhd->khd/dot_general | solution.py:192
  388.1 3.8 fusion.111
  391.9 8.4 %fusion.98 = bf16[12,64,512]{2,1,0:T(8,128)(2,1)} fusion(bf16[512,12,64]{0,2,1:T(8,128)(2,1)S(1)} %bitcast.187, f32[12,512]{1,0:T(8,128)S(1)} %copy-done.117, f32[12,512,512]{1,2,0:T(8,128)} %copy-done.2, pred[512,512]{0,1:T(8,128)(4,1)S(1)} %copy-done.35), kind=kOutput, calls=%fused_computation.201 | convolution fusion | flops 415629312 | bytes 14442496 | tf_op jit(solution)/shard_map/hqk,qhd->khd/dot_general | solution.py:192
  400.3 6.5 fusion.113
  406.8 3.9 fusion.104
  410.8 9.6 %add_add_fusion.1 = f32[768,2304]{1,0:T(8,128)} fusion(f32[768,2304]{1,0:T(8,128)} %fusion.113, f32[768,2304]{1,0:T(8,128)S(1)} %fusion.111, bf16[512,768]{0,1:T(8,128)(2,1)} %bitcast.212, bf16[512,768]{0,1:T(8,128)(2,1)} %bitcast.196, bf16[512,768]{0,1:T(8,128)(2,1)S(1)} %bitcast.194, f32[512]{0:T(512)S(1)} %copy-done.136, f32[512]{0:T(512)S(1)} %copy-done.134, ...), kind=kOutput, calls=%fused_computation.25 | convolution fusion | flops 1824522240 | bytes 24387584 | tf_op jit(solution)/shard_map/dot_general | solution.py:60
  420.6 4.9 fusion.112
  427.8 5.7 fusion.73
  437.0 3.8 fusion.65
  447.2 25.5 %reduce-scatter.12.cloned.1.call-done = f32[48,2304]{1,0:T(8,128)} async-done(((f32[768,2304]{1,0:T(8,128)}), f32[48,2304]{1,0:T(8,128)}) %reduce-scatter.12.cloned.1.call-update) | async-done | bytes 442384 | tf_op jit(solution)/shard_map/reduce_scatter | solution.py:287
  472.8 93.5 %reduce-scatter.8.cloned.1.call-done = f32[48,2304]{1,0:T(8,128)} async-done(((f32[768,2304]{1,0:T(8,128)}), f32[48,2304]{1,0:T(8,128)}) %reduce-scatter.8.cloned.1.call-update) | async-done | bytes 442384 | tf_op jit(solution)/shard_map/reduce_scatter | solution.py:285
  566.4 3.5 fusion.72
  572.5 53.4 %reduce-scatter.16.cloned.1.call-done = f32[48,2]{1,0:T(8,128)} async-done(((f32[768,2]{1,0:T(8,128)}), f32[48,2]{1,0:T(8,128)}) %reduce-scatter.16.cloned.1.call-update) | async-done | bytes 400
  626.7 4.9 psum.44
  632.2 40.1 %all-reduce.3.cloned.1.call-done = (f32[48,2304]{1,0:T(8,128)}, f32[48,768]{1,0:T(8,128)}, f32[48,2304]{1,0:T(8,128)}, f32[72,768]{1,0:T(8,128)}) async-done(((f32[48,2304]{1,0:T(8,128)}, f32[48,768]{1,0:T(8,128)}, f32[48,2304]{1,0:T(8,128)}, f32[72,768]{1,0:T(8,128)}), (f32[48,2304]{1,0:T(8,128)}, f32[48,768]{1,0:T(8,128)}, f32[48,2304]{1,0:T(8,128)}, f32[72,768]{1,0:T(8,128)})) %all-reduce.3.cloned.1.call-update) | async-done | bytes 1253392 | tf_op jit(solution)/shard_map/psum | solution.py:283
  (544 shorter events, 168.9 us)
Async XLA Ops:
  7.2 53.7 %all-gather.6.cloned.1.call-start = ((), (), s32[]{:S(2)}) async-start(), calls=%async_computation.5 | async-start | bytes 3760128 | tf_op jit(solution)/shard_map/all_gather | solution.py:261
  9.1 111.6 %all-gather.8.cloned.1.call-start = ((), (), s32[]{:S(2)}) async-start(), calls=%async_computation.6 | async-start | bytes 1253376 | tf_op jit(solution)/shard_map/all_gather | solution.py:262
  10.8 153.9 %all-gather.10.cloned.1.call-start = ((), (), s32[]{:S(2)}) async-start(), calls=%async_computation.7 | async-start | bytes 3760128 | tf_op jit(solution)/shard_map/all_gather | solution.py:263
  12.6 178.3 %all-gather.12.cloned.1.call-start = ((), (), s32[]{:S(2)}) async-start(), calls=%async_computation.8 | async-start | bytes 1880064 | tf_op jit(solution)/shard_map/all_gather | solution.py:264
  13.4 433.9 %reduce-scatter.10.cloned.1.call-start = ((), (), s32[]{:S(2)}) async-start(), calls=%async_computation.10 | async-start | bytes 2506752 | tf_op jit(solution)/shard_map/reduce_scatter | solution.py:286
  14.4 98.6 %copy-start.31 = (pred[512,512]{0,1:T(8,128)(4,1)}, pred[512,512]{0,1:T(8,128)(4,1)S(1)}, u32[]{:S(2)}) copy-start(pred[512,512]{0,1:T(8,128)(4,1)S(1)} %broadcast_compare_fusion) | copy-start | bytes 786436
  17.3 56.1 %copy-start.143 = (f32[512]{0:T(512)}, f32[512]{0:T(512)S(1)}, u32[]{:S(2)}) copy-start(f32[512]{0:T(512)S(1)} %broadcast_multiply_fusion.26) | copy-start | bytes 6148
  17.3 43.5 %copy-start.133 = (f32[512]{0:T(512)}, f32[512]{0:T(512)S(1)}, u32[]{:S(2)}) copy-start(f32[512]{0:T(512)S(1)} %get-tuple-element.178) | copy-start | bytes 6148
  17.3 50.5 %copy-start.147 = (f32[512]{0:T(512)}, f32[512]{0:T(512)S(1)}, u32[]{:S(2)}) copy-start(f32[512]{0:T(512)S(1)} %get-tuple-element.179) | copy-start | bytes 6148
  18.2 55.2 %copy-start.149 = (f32[512]{0:T(512)}, f32[512]{0:T(512)S(1)}, u32[]{:S(2)}) copy-start(f32[512]{0:T(512)S(1)} %add_rsqrt_fusion.5) | copy-start | bytes 6148
  41.5 31.9 %copy-start.124 = (f32[768]{0:T(1024)}, f32[768]{0:T(1024)S(1)}, u32[]{:S(2)}) copy-start(f32[768]{0:T(1024)S(1)} %get-tuple-element.46) | copy-start | bytes 9220
  42.5 22.5 %copy-start.135 = (f32[512]{0:T(512)}, f32[512]{0:T(512)S(1)}, u32[]{:S(2)}) copy-start(f32[512]{0:T(512)S(1)} %add_rsqrt_fusion.1) | copy-start | bytes 6148
  43.5 24.3 %copy-start.152 = (f32[512]{0:T(512)}, f32[512]{0:T(512)S(1)}, u32[]{:S(2)}) copy-start(f32[512]{0:T(512)S(1)} %add_rsqrt_fusion.3) | copy-start | bytes 6148
  123.1 81.8 %copy-start.137 = (f32[512]{0:T(512)}, f32[512]{0:T(512)S(1)}, u32[]{:S(2)}) copy-start(f32[512]{0:T(512)S(1)} %broadcast_multiply_fusion.21) | copy-start | bytes 6148
  138.3 8.9 %copy-start.50 = (bf16[512,768]{0,1:T(8,128)(2,1)}, bf16[512,768]{0,1:T(8,128)(2,1)S(1)}, u32[]{:S(2)}) copy-start(bf16[512,768]{0,1:T(8,128)(2,1)S(1)} %copy.157) | copy-start | bytes 2359300
  154.5 50.4 %copy-start.140 = (f32[512]{0:T(512)}, f32[512]{0:T(512)S(1)}, u32[]{:S(2)}) copy-start(f32[512]{0:T(512)S(1)} %add_rsqrt_fusion.2) | copy-start | bytes 6148
  164.7 102.3 %copy-start.116 = (f32[12,512]{1,0:T(8,128)}, f32[12,512]{1,0:T(8,128)S(1)}, u32[]{:S(2)}) copy-start(f32[12,512]{1,0:T(8,128)S(1)} %log_add_fusion.2) | copy-start | bytes 73732
  221.4 12.1 %copy-start.7 = (f32[512,768]{1,0:T(8,128)}, f32[512,768]{1,0:T(8,128)S(1)}, u32[]{:S(2)}) copy-start(f32[512,768]{1,0:T(8,128)S(1)} %get-tuple-element.165) | copy-start | bytes 4718596
  245.7 201.6 %reduce-scatter.14.cloned.1.call-start = ((), (), s32[]{:S(2)}) async-start(), calls=%async_computation.12 | async-start | bytes 3760128 | tf_op jit(solution)/shard_map/reduce_scatter | solution.py:288
  252.9 61.5 %copy-start.118 = (f32[12,512]{1,0:T(8,128)}, f32[12,512]{1,0:T(8,128)S(1)}, u32[]{:S(2)}) copy-start(f32[12,512]{1,0:T(8,128)S(1)} %log_add_fusion.1) | copy-start | bytes 73732
  252.9 14.1 %slice-start.6 = ((s8[12582912]{0:T(1024)(128)(4,1)}), s8[4194304]{0:T(1024)(128)(4,1)S(1)}, s32[]{:S(2)}) async-start(s8[12582912]{0:T(1024)(128)(4,1)} %bitcast.168), calls=%async_computation.21 | async-start | bytes 8388608
  252.9 14.1 %slice-start.7 = ((s8[12582912]{0:T(1024)(128)(4,1)}), s8[4194304]{0:T(1024)(128)(4,1)S(1)}, s32[]{:S(2)}) async-start(s8[12582912]{0:T(1024)(128)(4,1)} %bitcast.168), calls=%async_computation.22 | async-start | bytes 8388608
  252.9 14.1 %slice-start.8 = ((s8[12582912]{0:T(1024)(128)(4,1)}), s8[4194304]{0:T(1024)(128)(4,1)S(1)}, s32[]{:S(2)}) async-start(s8[12582912]{0:T(1024)(128)(4,1)} %bitcast.168), calls=%async_computation.23 | async-start | bytes 8388608
  252.9 14.1 %copy-start.34 = (pred[512,512]{0,1:T(8,128)(4,1)S(1)}, pred[512,512]{0,1:T(8,128)(4,1)}, u32[]{:S(2)}) copy-start(pred[512,512]{0,1:T(8,128)(4,1)} %broadcast_compare_fusion.2) | copy-start | bytes 786436
  281.0 191.8 %reduce-scatter.12.cloned.1.call-start = ((), (), s32[]{:S(2)}) async-start(), calls=%async_computation.11 | async-start | bytes 7520256 | tf_op jit(solution)/shard_map/reduce_scatter | solution.py:287
  289.7 17.8 %slice-start.3 = ((s8[12582912]{0:T(1024)(128)(4,1)}), s8[4194304]{0:T(1024)(128)(4,1)S(1)}, s32[]{:S(2)}) async-start(s8[12582912]{0:T(1024)(128)(4,1)} %bitcast.166), calls=%async_computation.18 | async-start | bytes 8388608
  295.5 12.0 %slice-start.4 = ((s8[12582912]{0:T(1024)(128)(4,1)}), s8[4194304]{0:T(1024)(128)(4,1)S(1)}, s32[]{:S(2)}) async-start(s8[12582912]{0:T(1024)(128)(4,1)} %bitcast.166), calls=%async_computation.19 | async-start | bytes 8388608
  314.4 11.4 %copy-start.139 = (f32[512]{0:T(512)S(1)}, f32[512]{0:T(512)}, u32[]{:S(2)}) copy-start(f32[512]{0:T(512)} %copy-done.137) | copy-start | bytes 6148
  314.4 11.4 %copy-start.146 = (f32[512]{0:T(512)S(1)}, f32[512]{0:T(512)}, u32[]{:S(2)}) copy-start(f32[512]{0:T(512)} %add_rsqrt_fusion) | copy-start | bytes 6148
  337.5 228.8 %reduce-scatter.8.cloned.1.call-start = ((), (), s32[]{:S(2)}) async-start(), calls=%async_computation.9 | async-start | bytes 7520256 | tf_op jit(solution)/shard_map/reduce_scatter | solution.py:285
  347.5 11.7 %slice-start = ((s8[12582912]{0:T(1024)(128)(4,1)}), s8[4194304]{0:T(1024)(128)(4,1)S(1)}, s32[]{:S(2)}) async-start(s8[12582912]{0:T(1024)(128)(4,1)} %bitcast.164), calls=%async_computation.15 | async-start | bytes 8388608
  348.1 11.0 %slice-start.1 = ((s8[12582912]{0:T(1024)(128)(4,1)}), s8[4194304]{0:T(1024)(128)(4,1)S(1)}, s32[]{:S(2)}) async-start(s8[12582912]{0:T(1024)(128)(4,1)} %bitcast.164), calls=%async_computation.16 | async-start | bytes 8388608
  348.1 11.0 %slice-start.2 = ((s8[12582912]{0:T(1024)(128)(4,1)}), s8[4194304]{0:T(1024)(128)(4,1)S(1)}, s32[]{:S(2)}) async-start(s8[12582912]{0:T(1024)(128)(4,1)} %bitcast.164), calls=%async_computation.17 | async-start | bytes 8388608
  420.3 205.5 %reduce-scatter.16.cloned.1.call-start = ((), (), s32[]{:S(2)}) async-start(), calls=%async_computation.13 | async-start | bytes 417792
  436.9 235.4 %all-reduce.3.cloned.1.call-start = ((), (), s32[]{:S(2)}) async-start(), calls=%async_computation.14 | async-start | bytes 2506752 | tf_op jit(solution)/shard_map/psum | solution.py:283
  445.6 120.7 %copy-start.160 = (f32[512]{0:T(512)S(1)}, f32[512]{0:T(512)}, u32[]{:S(2)}) copy-start(f32[512]{0:T(512)} %get-tuple-element.29) | copy-start | bytes 6148
  445.6 120.7 %copy-start.151 = (f32[512]{0:T(512)S(1)}, f32[512]{0:T(512)}, u32[]{:S(2)}) copy-start(f32[512]{0:T(512)} %copy-done.149) | copy-start | bytes 6148
  445.6 120.7 %copy-start.154 = (f32[512]{0:T(512)S(1)}, f32[512]{0:T(512)}, u32[]{:S(2)}) copy-start(f32[512]{0:T(512)} %broadcast_multiply_fusion.10) | copy-start | bytes 6148
  445.6 120.7 %copy-start.155 = (f32[512]{0:T(512)S(1)}, f32[512]{0:T(512)}, u32[]{:S(2)}) copy-start(f32[512]{0:T(512)} %broadcast_multiply_fusion.17) | copy-start | bytes 6148
  569.9 61.7 %copy-start.163 = (f32[48,2]{0,1:T(2,128)S(1)}, f32[48,2]{0,1:T(2,128)}, u32[]{:S(2)}) copy-start(f32[48,2]{0,1:T(2,128)} %param.25) | copy-start | bytes 1156
  569.9 61.7 %copy-start.164 = (f32[48,2]{0,1:T(2,128)S(1)}, f32[48,2]{0,1:T(2,128)}, u32[]{:S(2)}) copy-start(f32[48,2]{0,1:T(2,128)} %param.34) | copy-start | bytes 1156
  569.9 61.7 %copy-start.165 = (f32[48,2]{0,1:T(2,128)S(1)}, f32[48,2]{0,1:T(2,128)}, u32[]{:S(2)}) copy-start(f32[48,2]{0,1:T(2,128)} %param.35) | copy-start | bytes 1156
  570.0 102.4 %copy-start.73 = (f32[48,2304]{1,0:T(8,128)S(1)}, f32[48,2304]{1,0:T(8,128)}, u32[]{:S(2)}) copy-start(f32[48,2304]{1,0:T(8,128)} %param.23) | copy-start | bytes 1327108
  570.0 102.4 %copy-start.107 = (f32[48,2304]{1,0:T(8,128)S(1)}, f32[48,2304]{1,0:T(8,128)}, u32[]{:S(2)}) copy-start(f32[48,2304]{1,0:T(8,128)} %param.30) | copy-start | bytes 1327108
  570.0 102.4 %copy-start.108 = (f32[48,2304]{1,0:T(8,128)S(1)}, f32[48,2304]{1,0:T(8,128)}, u32[]{:S(2)}) copy-start(f32[48,2304]{1,0:T(8,128)} %param.31) | copy-start | bytes 1327108
  572.5 102.2 %copy-start.74 = (f32[48,2304]{1,0:T(8,128)S(1)}, f32[48,2304]{1,0:T(8,128)}, u32[]{:S(2)}) copy-start(f32[48,2304]{1,0:T(8,128)} %param.21) | copy-start | bytes 1327108
  572.5 102.2 %copy-start.109 = (f32[48,2304]{1,0:T(8,128)S(1)}, f32[48,2304]{1,0:T(8,128)}, u32[]{:S(2)}) copy-start(f32[48,2304]{1,0:T(8,128)} %param.26) | copy-start | bytes 1327108
  572.5 102.2 %copy-start.110 = (f32[48,2304]{1,0:T(8,128)S(1)}, f32[48,2304]{1,0:T(8,128)}, u32[]{:S(2)}) copy-start(f32[48,2304]{1,0:T(8,128)} %param.27) | copy-start | bytes 1327108
  (153 other events, 553.5 us)
Sparse Core Ops, SparseCore 0:
  10.9 49.9 all-gather.5
  63.1 37.3 all-gather.7
  103.4 46.0 all-gather.9
  151.5 39.3 all-gather.11
  245.8 61.5 reduce-scatter.9
  312.2 67.1 reduce-scatter.13
  383.9 88.8 reduce-scatter.11
  476.8 89.4 reduce-scatter.7
  570.8 55.0 reduce-scatter.15
  628.2 44.0 all-reduce.2
where the time goes:
time: 689 us; the launch traced here: 685 us
  waiting for transfers between devices  245 us (36%)
  matrix products  223 us (32%)
  other arithmetic  107 us (16%)
  local copies, waits for them, and re-layouts  64.1 us (9%)
  blocking collectives  28.1 us (4%)
  between operations  16.5 us (2%)
    reduce_scatter x1, waiting for transfers between devices, local(): lax.psum_scatter(summed[0], 'dp', scatter_dimension=0, tiled=True)  93.5 us
    dot_general x12, matrix products, contract_rows(): lax.dot_general(left, right, (((0,), (0,)), ((), ())), preferred_element_...  54.9 us
    unnamed x11, waiting for transfers between devices  53.5 us
    dot_general x12, matrix products, contract_cols(): lax.dot_general(left, right, (((1,), (1,)), ((), ())), preferred_element_...  45 us
    psum x1, waiting for transfers between devices, local(): summed = lax.psum((acc_q, acc_a, acc_i, acc_o, acc_g), 'rep')  40.1 us
    dot_general x3, matrix products, backward_pass(): jnp.einsum('qhd,khd->hqk', grad_ctx, v_low, preferred_element_type=jnp.fl...  32 us
    neg x12, other arithmetic, rotate_half(): -values[..., half_dim:]  26.5 us
    reduce_scatter x1, waiting for transfers between devices, local(): lax.psum_scatter(summed[2], 'dp', scatter_dimension=0, tiled=True)  25.5 us
  transfers between devices with their start and end apart: 10, of which 6 were waited for; matrix products, arithmetic and copies ran while one was open for 46% of the time, Pallas kernels for 0%

commit v1 on v0

v1 whole, which is shorter than its diff:
```python
import functools
import math

import jax
import jax.numpy as jnp
from jax import lax
from jax.experimental import pallas as pl
from jax.experimental.pallas import tpu as pltpu
from jax.sharding import PartitionSpec as P

HEADS = 12
HEAD_DIM = 64
STEP = 10
PAIR = 2 * HEAD_DIM
PAIRS = HEADS // 2

beta_one = 0.9
beta_two = 0.98
adam_eps = 1e-06
decay_rate = 1e-05
inv_root_two = 0.7071067811865476
inv_root_tau = 0.3989422804014327


def normalize(values):
    centred = values - jnp.mean(values, -1, keepdims=True)
    inv_std = lax.rsqrt(jnp.mean(centred * centred, -1, keepdims=True) + 1e-05)
    return (centred * inv_std, inv_std)


def norm_back(grad_out, x_hat, inv_std, gain_col):
    scaled = grad_out * gain_col
    return inv_std * (
        scaled
        - jnp.mean(scaled, -1, keepdims=True)
        - x_hat * jnp.mean(scaled * x_hat, -1, keepdims=True)
    )


def rope_tables(positions):
    freq_idx = jnp.arange(HEAD_DIM // 2).astype(jnp.float32)
    inv_freq = jnp.exp(freq_idx * (-2.0 * math.log(160000.0) / HEAD_DIM))
    angles = positions.astype(jnp.float32)[:, None] * inv_freq[None, :]
    cos, sin = jnp.cos(angles), jnp.sin(angles)
    return (
        jnp.concatenate([cos, cos, cos, cos], -1),
        jnp.concatenate([-sin, sin, -sin, sin], -1),
    )


def segments(lengths, row_count):
    ends = jnp.cumsum(lengths, -1)
    row_idx = jnp.arange(row_count)
    seg_ids = jnp.sum((row_idx[None, :, None] >= ends[:, None, :]).astype(jnp.int32), -1)
    starts = ends - lengths
    pick = seg_ids[:, :, None] == jnp.arange(lengths.shape[1])[None, None, :]
    positions = row_idx[None, :] - jnp.sum(jnp.where(pick, starts[:, None, :], 0), -1)
    return (seg_ids, positions)


def contract_rows(left, right):
    return lax.dot_general(
        left, right, (((0,), (0,)), ((), ())), preferred_element_type=jnp.float32
    )


def contract_cols(left, right):
    return lax.dot_general(
        left, right, (((1,), (1,)), ((), ())), preferred_element_type=jnp.float32
    )


def lanes_of(shape):
    return lax.broadcasted_iota(jnp.int32, shape, 1)


def swap_halves(values):
    lane = lanes_of(values.shape)
    up = pltpu.roll(values, PAIR - HEAD_DIM // 2, 1)
    down = pltpu.roll(values, HEAD_DIM // 2, 1)
    return jnp.where(lane % HEAD_DIM < HEAD_DIM // 2, up, down)


def mask_lanes(seg_col, lane):
    own = (lane % HEAD_DIM) == seg_col
    key_side = jnp.where(own, 1.0, 0.0).astype(jnp.bfloat16)
    few = lane % HEAD_DIM < 8
    query_side = jnp.where(few & jnp.logical_not(own), -1e30, 0.0).astype(jnp.bfloat16)
    return (query_side, key_side)


def attn_fwd_kernel(q_ref, k_ref, v_ref, cos_ref, sin_ref, seg_ref, rot_ref, ctx_ref):
    pair = pl.program_id(1)
    width = ctx_ref.shape[1] * PAIRS
    cos, sin = cos_ref[...], sin_ref[...]
    q_raw, k_raw = q_ref[...], k_ref[...]
    q_rot = ((q_raw * cos + swap_halves(q_raw) * sin) * 0.125).astype(jnp.bfloat16)
    k_rot = (k_raw * cos + swap_halves(k_raw) * sin).astype(jnp.bfloat16)
    v_low = v_ref[...].astype(jnp.bfloat16)
    at = pl.multiple_of(pair * PAIR, PAIR)
    rot_ref[:, pl.ds(at, PAIR)] = q_rot
    rot_ref[:, pl.ds(at + width, PAIR)] = k_rot
    rot_ref[:, pl.ds(at + 2 * width, PAIR)] = v_low
    lane = lanes_of(q_raw.shape)
    query_side, key_side = mask_lanes(seg_ref[...], lane)
    parts = []
    for head in range(2):
        own = (lane // HEAD_DIM) == head
        q_h = jnp.where(own, q_rot, query_side)
        k_h = jnp.where(own, k_rot, key_side)
        scores = contract_cols(q_h, k_h)
        expo = jnp.exp(scores - jnp.max(scores, -1, keepdims=True))
        total = jnp.sum(expo, -1, keepdims=True)
        probs = (expo * (1.0 / total)).astype(jnp.bfloat16)
        parts.append(jnp.dot(probs, v_low, preferred_element_type=jnp.float32))
    ctx_ref[...] = jnp.where(lane < HEAD_DIM, parts[0], parts[1]).astype(jnp.bfloat16)


def attn_bwd_kernel(q_ref, k_ref, v_ref, dctx_ref, cos_ref, sin_ref, seg_ref, out_ref):
    step = pl.program_id(1)
    width = out_ref.shape[1] // 3
    q_rot, k_rot, v_low, dctx = q_ref[...], k_ref[...], v_ref[...], dctx_ref[...]
    lane = lanes_of(q_rot.shape)
    query_side, key_side = mask_lanes(seg_ref[...], lane)
    k_turned = k_rot.astype(jnp.float32).T.astype(jnp.bfloat16)
    dq_parts, dk_parts, dv_parts = [], [], []
    for head in range(2):
        own = (lane // HEAD_DIM) == head
        q_h = jnp.where(own, q_rot, query_side)
        k_h = jnp.where(own, k_rot, key_side)
        v_h = jnp.where(own, v_low, jnp.zeros_like(v_low))
        scores = contract_cols(k_h, q_h)
        expo = jnp.exp(scores - jnp.max(scores, 0, keepdims=True))
        total = jnp.sum(expo, 0, keepdims=True)
        probs = expo * (1.0 / total)
        grad_probs = contract_cols(v_h, dctx)
        weighted = probs * grad_probs
        row_dots = jnp.sum(weighted, 0, keepdims=True)
        grad_scores = (weighted - probs * row_dots).astype(jnp.bfloat16)
        probs_low = probs.astype(jnp.bfloat16)
        dk_parts.append(jnp.dot(grad_scores, q_rot, preferred_element_type=jnp.float32))
        dv_parts.append(jnp.dot(probs_low, dctx, preferred_element_type=jnp.float32))
        dq_parts.append(
            jnp.dot(
                k_turned[head * HEAD_DIM : (head + 1) * HEAD_DIM],
                grad_scores,
                preferred_element_type=jnp.float32,
            )
        )
    cos, sin = cos_ref[...], sin_ref[...]
    dq = jnp.concatenate(dq_parts, 0).T * 0.125
    dk = jnp.where(lane < HEAD_DIM, dk_parts[0], dk_parts[1])
    dv = jnp.where(lane < HEAD_DIM, dv_parts[0], dv_parts[1])
    at = pl.multiple_of(step * PAIR, PAIR)
    out_ref[:, pl.ds(at, PAIR)] = (dq * cos - swap_halves(dq) * sin).astype(jnp.bfloat16)
    out_ref[:, pl.ds(at + width, PAIR)] = (dk * cos - swap_halves(dk) * sin).astype(jnp.bfloat16)
    out_ref[:, pl.ds(at + 2 * width, PAIR)] = dv.astype(jnp.bfloat16)


def attn_forward(qkv_all, cos_tab, sin_tab, seg_col, micro):
    rows = qkv_all.shape[0] // micro
    width = qkv_all.shape[1] // 3
    table = pl.BlockSpec((rows, PAIR), lambda m, p: (m, 0))
    return pl.pallas_call(
        attn_fwd_kernel,
        grid=(micro, PAIRS),
        in_specs=[
            pl.BlockSpec((rows, PAIR), lambda m, p: (m, p)),
            pl.BlockSpec((rows, PAIR), lambda m, p: (m, PAIRS + p)),
            pl.BlockSpec((rows, PAIR), lambda m, p: (m, 2 * PAIRS + p)),
            table,
            table,
            table,
        ],
        out_specs=[
            pl.BlockSpec((rows, 3 * width), lambda m, p: (m, 0)),
            pl.BlockSpec((rows, PAIR), lambda m, p: (m, p)),
        ],
        out_shape=[
            jax.ShapeDtypeStruct(qkv_all.shape, jnp.bfloat16),
            jax.ShapeDtypeStruct((qkv_all.shape[0], width), jnp.bfloat16),
        ],
        compiler_params=pltpu.CompilerParams(vmem_limit_bytes=40 * 1024 * 1024),
        cost_estimate=pl.CostEstimate(
            flops=micro * HEADS * 4 * rows * rows * PAIR,
            bytes_accessed=qkv_all.size * 7,
            transcendentals=micro * HEADS * rows * rows,
        ),
    )(qkv_all, qkv_all, qkv_all, cos_tab, sin_tab, seg_col)


def attn_backward(rot, dctx, cos_tab, sin_tab, seg_col, micro, first, count):
    rows = rot.shape[0] // micro
    table = pl.BlockSpec((rows, PAIR), lambda m, p: (m, 0))
    return pl.pallas_call(
        attn_bwd_kernel,
        grid=(micro, count),
        in_specs=[
            pl.BlockSpec((rows, PAIR), lambda m, p: (m, first + p)),
            pl.BlockSpec((rows, PAIR), lambda m, p: (m, PAIRS + first + p)),
            pl.BlockSpec((rows, PAIR), lambda m, p: (m, 2 * PAIRS + first + p)),
            pl.BlockSpec((rows, PAIR), lambda m, p: (m, first + p)),
            table,
            table,
            table,
        ],
        out_specs=pl.BlockSpec((rows, 3 * count * PAIR), lambda m, p: (m, 0)),
        out_shape=jax.ShapeDtypeStruct((rot.shape[0], 3 * count * PAIR), jnp.bfloat16),
        compiler_params=pltpu.CompilerParams(vmem_limit_bytes=40 * 1024 * 1024),
        cost_estimate=pl.CostEstimate(
            flops=micro * count * 20 * rows * rows * PAIR,
            bytes_accessed=rot.shape[0] * count * PAIR * 14,
            transcendentals=micro * count * 2 * rows * rows,
        ),
    )(rot, rot, rot, dctx, cos_tab, sin_tab, seg_col)


def adam_update(weight, first, second, grad, rate):
    first_new = beta_one * first + (1.0 - beta_one) * grad
    second_new = beta_two * second + (1.0 - beta_two) * grad * grad
    corr_one = 1.0 - beta_one**STEP
    corr_two = 1.0 - beta_two**STEP
    direction = first_new / corr_one / (jnp.sqrt(second_new / corr_two) + adam_eps)
    return (weight - rate * (direction + decay_rate * weight), first_new, second_new)


def local(
    rep_size,
    tokens,
    cotangent,
    lengths,
    qkv_weight,
    attn_out_weight,
    mlp_in_weight,
    mlp_out_weight,
    norm_gains,
    qkv_first,
    qkv_second,
    attn_first,
    attn_second,
    mlp_in_first,
    mlp_in_second,
    mlp_out_first,
    mlp_out_second,
    gains_first,
    gains_second,
):
    micro = lengths.shape[0]
    rows = tokens.shape[0] // micro
    width = tokens.shape[1]
    ff_width = mlp_in_weight.shape[1] // 2

    def gather(value):
        return lax.all_gather(value, "dp", axis=0, tiled=True)

    def reduce_owned(value):
        part = lax.psum_scatter(value, "dp", scatter_dimension=0, tiled=True)
        other = lax.ppermute(part, "rep", [(i, rep_size - 1 - i) for i in range(rep_size)])
        return part.astype(jnp.float32) + other.astype(jnp.float32)

    padded_gains = jnp.pad(norm_gains, ((0, 0), (0, 126)))
    packed = gather(jnp.concatenate([qkv_weight, padded_gains], 1).astype(jnp.bfloat16))
    w_attn = gather(attn_out_weight.astype(jnp.bfloat16))
    w_in = gather(mlp_in_weight.astype(jnp.bfloat16))
    w_out = gather(mlp_out_weight.astype(jnp.bfloat16))
    w_qkv = packed[:, : 3 * width]
    gain_one = packed[:, 3 * width].astype(jnp.float32)
    gain_two = packed[:, 3 * width + 1].astype(jnp.float32)

    seg_ids, positions = segments(lengths, rows)
    cos_tab, sin_tab = rope_tables(positions.reshape(-1))
    seg_col = jnp.broadcast_to(seg_ids.reshape(-1, 1), (micro * rows, PAIR))

    x_float = tokens.astype(jnp.float32)
    hat_one, inv_one = normalize(x_float)
    h_one = (hat_one * gain_one).astype(jnp.bfloat16)
    qkv_all = jnp.dot(h_one, w_qkv, preferred_element_type=jnp.float32)
    rot, context = attn_forward(qkv_all, cos_tab, sin_tab, seg_col, micro)
    middle = x_float + jnp.dot(context, w_attn, preferred_element_type=jnp.float32)
    hat_two, inv_two = normalize(middle)
    h_two = (hat_two * gain_two).astype(jnp.bfloat16)
    gate_up = jnp.dot(h_two, w_in, preferred_element_type=jnp.float32)
    act_in = gate_up[:, :ff_width]
    gate_in = gate_up[:, ff_width:]
    cdf_vals = 0.5 * (1.0 + lax.erf(act_in * inv_root_two))
    act_out = act_in * cdf_vals
    hidden = (act_out * gate_in).astype(jnp.bfloat16)

    grad_float = cotangent.astype(jnp.float32)
    grad_hidden = contract_cols(cotangent, w_out)
    grad_wo = contract_rows(hidden, cotangent).astype(jnp.bfloat16)
    sum_o = reduce_owned(grad_wo)
    activations = (middle + jnp.dot(hidden, w_out, preferred_element_type=jnp.float32)).astype(
        jnp.bfloat16
    )
    grad_act = (
        grad_hidden * gate_in * (cdf_vals + act_in * inv_root_tau * jnp.exp(-0.5 * act_in * act_in))
    )
    grad_gate = grad_hidden * act_out
    grad_gu = jnp.concatenate([grad_act, grad_gate], 1).astype(jnp.bfloat16)
    sum_i = reduce_owned(contract_rows(h_two, grad_gu).astype(jnp.bfloat16))
    grad_h_two = contract_cols(grad_gu, w_in)
    grad_mid = grad_float + norm_back(grad_h_two, hat_two, inv_two, gain_two)
    grad_g_two = jnp.sum(grad_h_two * hat_two, 0)
    grad_mid_low = grad_mid.astype(jnp.bfloat16)
    sum_a = reduce_owned(contract_rows(context, grad_mid_low).astype(jnp.bfloat16))
    grad_ctx = contract_cols(grad_mid_low, w_attn).astype(jnp.bfloat16)

    half = PAIRS // 2
    side = half * PAIR
    grads_qkv, sums_q = [], []
    grad_h_one = None
    for part in range(2):
        grad_qkv = attn_backward(
            rot, grad_ctx, cos_tab, sin_tab, seg_col, micro, part * half, half
        )
        w_part = jnp.concatenate(
            [
                w_qkv[:, n * width + part * side : n * width + (part + 1) * side]
                for n in range(3)
            ],
            1,
        )
        term = contract_cols(grad_qkv, w_part)
        grad_h_one = term if grad_h_one is None else grad_h_one + term
        grad_wq = contract_rows(h_one, grad_qkv).astype(jnp.bfloat16)
        if part == 0:
            sums_q.append(reduce_owned(grad_wq))
    grad_g_one = jnp.sum(grad_h_one * hat_one, 0)
    grad_gains = jnp.stack([grad_g_one, grad_g_two], 1).astype(jnp.bfloat16)
    tail = reduce_owned(
        jnp.concatenate([grad_wq, jnp.pad(grad_gains, ((0, 0), (0, 126)))], 1)
    )
    sums_q.append(tail[:, : 3 * side])
    sum_g = tail[:, 3 * side : 3 * side + 2]
    input_grad = grad_mid + norm_back(grad_h_one, hat_one, inv_one, gain_one)
    sum_q = jnp.concatenate(
        [sums_q[part][:, n * side : (n + 1) * side] for n in range(3) for part in range(2)], 1
    )

    qkv_res = adam_update(qkv_weight, qkv_first, qkv_second, sum_q, 0.03)
    attn_res = adam_update(attn_out_weight, attn_first, attn_second, sum_a, 0.3)
    in_res = adam_update(mlp_in_weight, mlp_in_first, mlp_in_second, sum_i, 0.03)
    out_res = adam_update(mlp_out_weight, mlp_out_first, mlp_out_second, sum_o, 0.03)
    gain_res = adam_update(norm_gains, gains_first, gains_second, sum_g, 0.5)
    return (activations, input_grad, *qkv_res, *attn_res, *in_res, *out_res, *gain_res)


def solution(mesh):
    rows_spec = P(("dp", "rep"), None)
    owned = P("dp", None)
    return jax.shard_map(
        functools.partial(local, mesh.shape["rep"]),
        mesh=mesh,
        in_specs=(rows_spec,) * 3 + (owned,) * 15,
        out_specs=(rows_spec,) * 2 + (owned,) * 15,
        check_vma=False,
    )
```

time: 689 us -> 574 us (0.83)
  matrix products: 223 us -> 104 us
  Pallas kernels: 0 us -> 77.1 us
  other arithmetic: 107 us -> 43.9 us
  blocking collectives: 28.1 us -> 0 us
    dot_general x30 -> x4, matrix products: 123 us -> 35.5 us  [the longest x1 11.8 us: local(): gate_up = jnp.dot(h_two, w_in, preferred_element_type=jnp.float32)]
    pallas_call x0 -> x3, Pallas kernels: none -> 77.1 us  [the longest x2 48.8 us: attn_backward(): pl.pallas_call(attn_bwd_kernel, grid=(micro, count), in_specs=[pl.BlockSp...]
    reduce_scatter x4 -> x3, waiting for transfers between devices: 119 us -> 47.8 us  [reduce_owned(): part = lax.psum_scatter(value, 'dp', scatter_dimension=0, tiled=True)]
    all_gather x4, waiting for transfers between devices: 32.3 us -> 98.5 us  [gather(): return lax.all_gather(value, 'dp', axis=0, tiled=True)]
    psum x1 -> x0, waiting for transfers between devices: 40.1 us -> none  [local(): summed = lax.psum((acc_q, acc_a, acc_i, acc_o, acc_g), 'rep')]
    unnamed x11, waiting for transfers between devices: 53.5 us -> 91.8 us
    unnamed x384 -> x89, local copies, waits for them, and re-layouts: 25.2 us -> 63.4 us
    slice x16 -> x1, local copies, waits for them, and re-layouts: 33 us -> 2.55 us  [local(): w_qkv[:, n * width + part * side:n * width + (part + 1) * side]]
  transfers between devices with their start and end apart: 10 -> 14, of which waited for: 6 -> 9; matrix products, arithmetic and copies ran while one was open for 46% -> 29% of each run, Pallas kernels for 0% -> 14%
where the time goes in v1:
time: 574 us; the launch traced here: 564 us
  waiting for transfers between devices  249 us (43%)
  matrix products  104 us (18%)
  Pallas kernels  77.1 us (13%)
  local copies, waits for them, and re-layouts  68.4 us (12%)
  other arithmetic  43.9 us (8%)
  between operations  14.9 us (3%)
  starting transfers between devices  7.04 us (1%)
    all_gather x4, waiting for transfers between devices, gather(): return lax.all_gather(value, 'dp', axis=0, tiled=True)  98.5 us
    unnamed x11, waiting for transfers between devices  91.8 us
    unnamed x89, local copies, waits for them, and re-layouts  63.4 us
    pallas_call x2, Pallas kernels, attn_backward(): pl.pallas_call(attn_bwd_kernel, grid=(micro, count), in_specs=[pl.BlockSp...  48.8 us
    reduce_scatter x3, waiting for transfers between devices, reduce_owned(): part = lax.psum_scatter(value, 'dp', scatter_dimension=0, tiled=True)  47.8 us
    dot_general x5, matrix products, contract_cols(): lax.dot_general(left, right, (((1,), (1,)), ((), ())), preferred_element_...  36.5 us
    dot_general x5, matrix products, contract_rows(): lax.dot_general(left, right, (((0,), (0,)), ((), ())), preferred_element_...  32.1 us
    pallas_call x1, Pallas kernels, attn_forward(): pl.pallas_call(attn_fwd_kernel, grid=(micro, PAIRS), in_specs=[pl.BlockSp...  28.2 us
  transfers between devices with their start and end apart: 14, of which 9 were waited for; matrix products, arithmetic and copies ran while one was open for 29% of the time, Pallas kernels for 14%

profile of v1, /device:TPU:0, one launch (start us, length us, event | category | flops | bytes accessed | tf_op | source)
XLA Modules:
  0.0 564.2 jit_solution(5655633883090496017)
XLA Ops:
  16.6 2.8 copy.187
  20.7 4.3 copy.191
  25.0 2.8 fusion.39
  29.1 32.3 %all-gather.5.cloned.1.call-done = bf16[768,2432]{1,0:T(8,128)(2,1)} async-done(((bf16[48,2432]{1,0:T(8,128)(2,1)}), bf16[768,2432]{1,0:T(8,128)(2,1)}) %all-gather.5.cloned.1.call-update) | async-done | bytes 3735568 | tf_op jit(solution)/shard_map/all_gather | solution.py:254
  62.7 11.5 %fusion.20.q_ref.k_ref.v_ref = f32[1536,2304]{1,0:T(8,128)} fusion(bf16[768,2432]{1,0:T(8,128)(2,1)} %all-gather.5.cloned.1.call-done, bf16[1536,768]{0,1:T(8,128)(2,1)} %copy-done.8, f32[768]{0:T(1024)S(1)} %get-tuple-element.147, f32[1536]{0:T(1024)S(1)} %add_rsqrt_fusion.1, f32[1536]{0:T(1024)S(1)} %broadcast_multiply_fusion.5), kind=kOutput, calls=%fused_computation.41 | convolution fusion | flops 5441716224 | bytes 20069376 | tf_op jit(solution)/shard_map/dot_general | solution.py:277
  74.4 28.2 %shard_map.305 = (bf16[1536,2304]{1,0:T(8,128)(2,1)S(1)}, bf16[1536,768]{1,0:T(8,128)(2,1)S(1)}) custom-call(f32[1536,2304]{1,0:T(8,128)} %fusion.20.q_ref.k_ref.v_ref, f32[1536,2304]{1,0:T(8,128)} %fusion.20.q_ref.k_ref.v_ref, f32[1536,2304]{1,0:T(8,128)} %fusion.20.q_ref.k_ref.v_ref, f32[1536,128]{1,0:T(8,128)S(1)} %get-tuple-element.179.cos_ref, ...), custom_call_target="tpu_custom_call" | custom-call | flops 4831838208 | bytes 24772608 | tf_op jit(solution)/shard_map/pallas_call | solution.py:164
  102.7 2.8 copy-done
  106.9 4.9 fusion.58
  111.8 2.2 copy-done.13
  114.6 36.1 %all-gather.9.cloned.1.call-done = bf16[768,2304]{1,0:T(8,128)(2,1)} async-done(((bf16[48,2304]{1,0:T(8,128)(2,1)}), bf16[768,2304]{1,0:T(8,128)(2,1)}) %all-gather.9.cloned.1.call-update) | async-done | bytes 3538960 | tf_op jit(solution)/shard_map/all_gather | solution.py:254
  150.6 11.8 %fusion.48 = f32[1536,2304]{1,0:T(8,128)} fusion(bf16[768,2304]{1,0:T(8,128)(2,1)} %all-gather.9.cloned.1.call-done, f32[1536,768]{0,1:T(8,128)} %copy-done.13, f32[768]{0:T(1024)S(1)} %get-tuple-element.146, f32[1536]{0:T(1024)S(1)} %add_rsqrt_fusion, f32[1536]{0:T(1024)S(1)} %broadcast_multiply_fusion.4), kind=kOutput, calls=%fused_computation.122 | convolution fusion | flops 5440536576 | bytes 22428672 | tf_op jit(solution)/shard_map/dot_general | solution.py:282
  162.5 30.2 %all-gather.11.cloned.1.call-done = bf16[1152,768]{1,0:T(8,128)(2,1)} async-done(((bf16[72,768]{1,0:T(8,128)(2,1)}), bf16[1152,768]{1,0:T(8,128)(2,1)}) %all-gather.11.cloned.1.call-update) | async-done | bytes 1769488 | tf_op jit(solution)/shard_map/all_gather | solution.py:254
  192.6 12.9 %fusion.4 = (bf16[1536,1152]{1,0:T(8,128)(2,1)}, bf16[1536,1152]{1,0:T(8,128)(2,1)}, bf16[1536,1152]{1,0:T(8,128)(2,1)}) fusion(f32[1536,2304]{1,0:T(8,128)} %fusion.48, bf16[1536,768]{1,0:T(8,128)(2,1)} %param.19, bf16[1152,768]{1,0:T(8,128)(2,1)} %all-gather.11.cloned.1.call-done), kind=kOutput, calls=%fused_computation.5 | convolution fusion | flops 2746220544 | bytes 28901376 | tf_op jit(solution)/shard_map/dot_general | solution.py:68
  205.6 9.3 %multiply_reduce_fusion = (bf16[768]{0:T(1024)(128)(2,1)S(1)}, f32[1536]{0:T(1024)S(1)}, f32[1536]{0:T(1024)S(1)}, f32[1536,768]{0,1:T(8,128)S(1)}) fusion(f32[1536,768]{0,1:T(8,128)S(1)} %copy-done.14, f32[1536]{0:T(1024)S(1)} %add_rsqrt_fusion, f32[1536]{0:T(1024)S(1)} %broadcast_multiply_fusion.4, f32[768]{0:T(1024)S(1)} %get-tuple-element.146, ...), kind=kOutput, calls=%fused_computation.28 | convolution fusion | flops 5459406848 | bytes 20083200 | tf_op jit(solution)/shard_map/dot_general | solution.py:68
  216.6 2.1 copy-done.12
  218.7 3.1 convolution_convert_fusion.5
  221.9 7.0 %convolution_convert_fusion.1 = bf16[1152,768]{1,0:T(8,128)(2,1)} fusion(bf16[1536,1152]{1,0:T(8,128)(2,1)} %get-tuple-element.165, bf16[1536,768]{1,0:T(8,128)(2,1)} %param.19), kind=kOutput, calls=%fused_computation.43 | convolution fusion | flops 2718793728 | bytes 7667712 | tf_op jit(solution)/shard_map/dot_general | solution.py:62
  229.0 4.9 convolution_convert_fusion.4.dctx_ref
  233.9 24.8 %shard_map.306 = bf16[1536,1152]{1,0:T(8,128)(2,1)S(1)} custom-call(bf16[1536,2304]{1,0:T(8,128)(2,1)} %copy-done, bf16[1536,2304]{1,0:T(8,128)(2,1)} %copy-done, bf16[1536,2304]{1,0:T(8,128)(2,1)} %copy-done, bf16[1536,768]{1,0:T(8,128)(2,1)S(1)} %convolution_convert_fusion.4.dctx_ref, f32[1536,128]{1,0:T(8,128)S(1)} %get-tuple-element.179.cos_ref, ...), custom_call_target="tpu_custom_call" | custom-call | flops 6039797760 | bytes 8257536 | tf_op jit(solution)/shard_map/pallas_call | solution.py:195
  260.5 4.6 convolution_convert_fusion.3
  265.1 2.6 fusion.57
  268.3 3.2 fusion.23
  271.6 24.0 %shard_map.307 = bf16[1536,1152]{1,0:T(8,128)(2,1)S(1)} custom-call(bf16[1536,2304]{1,0:T(8,128)(2,1)} %copy-done, bf16[1536,2304]{1,0:T(8,128)(2,1)} %copy-done, bf16[1536,2304]{1,0:T(8,128)(2,1)} %copy-done, bf16[1536,768]{1,0:T(8,128)(2,1)S(1)} %copy-done.2, f32[1536,128]{1,0:T(8,128)S(1)} %get-tuple-element.179.cos_ref, ...), custom_call_target="tpu_custom_call" | custom-call | flops 6039797760 | bytes 8257536 | tf_op jit(solution)/shard_map/pallas_call | solution.py:195
  295.6 6.2 %fusion.16 = (bf16[768]{0:T(1024)(128)(2,1)S(1)}, f32[1536]{0:T(1024)}, f32[1536]{0:T(1024)}, f32[1536,768]{0,1:T(8,128)}) fusion(bf16[1536,768]{0,1:T(8,128)(2,1)S(1)} %copy-done.10, f32[1536]{0:T(1024)S(1)} %add_rsqrt_fusion.1, f32[1536]{0:T(1024)S(1)} %broadcast_multiply_fusion.5, f32[768]{0:T(1024)S(1)} %get-tuple-element.147, ...), kind=kOutput, calls=%fused_computation.26 | convolution fusion | flops 2735010048 | bytes 17134080 | tf_op jit(solution)/shard_map/dot_general | solution.py:68
  302.1 5.3 convolution_convert_fusion.2
  310.6 2.4 copy.200
  313.0 2.4 copy.201
  315.4 2.4 copy.205
  317.8 2.4 copy.194
  320.2 2.4 copy.198
  325.2 12.1 %convolution_convert_fusion = bf16[768,2304]{1,0:T(8,128)(2,1)} fusion(bf16[1536,1152]{1,0:T(8,128)(2,1)} %get-tuple-element.164, bf16[1536,1152]{1,0:T(8,128)(2,1)} %get-tuple-element.163, f32[1536,768]{0,1:T(8,128)} %copy-done.13, f32[768]{0:T(1024)} %copy-done.27, f32[1536]{0:T(1024)} %copy-done.25, f32[1536]{0:T(1024)S(1)} %broadcast_multiply_fusion.4), kind=kOutput, calls=%fused_computation.20 | convolution fusion | flops 5456461824 | bytes 15350784 | tf_op jit(solution)/shard_map/dot_general | solution.py:62
  338.0 7.6 %fusion.15 = f32[1536,768]{0,1:T(8,128)} fusion(f32[1536,768]{0,1:T(8,128)} %copy-done.12, bf16[1536,768]{0,1:T(8,128)(2,1)S(1)} %copy-done.11, f32[1536,768]{0,1:T(8,128)} %get-tuple-element.178, f32[1536]{0:T(1024)} %broadcast_multiply_fusion, f32[1536]{0:T(1024)} %broadcast_multiply_fusion.1, f32[768]{0:T(1024)} %copy-done.26, f32[1536]{0:T(1024)S(1)} %copy-done.24, ...), kind=kLoop, calls=%fused_computation.25 | loop fusion | flops 10616832 | bytes 16542720 | tf_op jit(solution)/shard_map/add | solution.py:336
  347.1 7.3 %add_convert_fusion = bf16[1536,768]{0,1:T(8,128)(2,1)S(1)} fusion(f32[1536,768]{0,1:T(8,128)} %copy-done.13, bf16[1536,1152]{1,0:T(8,128)(2,1)} %get-tuple-element.165, bf16[1152,768]{1,0:T(8,128)(2,1)} %all-gather.11.cloned.1.call-done), kind=kOutput, calls=%fused_computation.31 | convolution fusion | flops 2720268288 | bytes 12386304 | tf_op jit(solution)/shard_map/dot_general | solution.py:293
  354.3 6.4 %copy.209 = f32[1536,768]{1,0:T(8,128)} copy(f32[1536,768]{0,1:T(8,128)} %fusion.15) | data formatting | bytes 9437184
  360.8 2.4 copy.208
  365.7 38.9 %reduce-scatter.16.cloned.1.call-done = bf16[48,1152]{1,0:T(8,128)(2,1)} async-done(((bf16[768,1152]{1,0:T(8,128)(2,1)}), bf16[48,1152]{1,0:T(8,128)(2,1)}) %reduce-scatter.16.cloned.1.call-update) | async-done | bytes 110608
  407.9 2.2 multiply_subtract_fusion.2
  410.1 3.7 collective-permute-done
  415.7 52.7 %reduce-scatter.18.cloned.1.call-done = bf16[48,1280]{1,0:T(8,128)(2,1)} async-done(((bf16[768,1280]{1,0:T(8,128)(2,1)}), bf16[48,1280]{1,0:T(8,128)(2,1)}) %reduce-scatter.18.cloned.1.call-update) | async-done | bytes 122896
  472.6 5.6 %collective-permute-done.1 = bf16[48,1280]{0,1:T(8,128)(2,1)S(1)} collective-permute-done((bf16[48,1280]{0,1:T(8,128)(2,1)}, bf16[48,1280]{0,1:T(8,128)(2,1)S(1)}, u32[]{:S(2)}, u32[]{:S(2)}) %collective-permute-start.1) | collective-permute-done | bytes 122912 | tf_op jit(solution)/shard_map/ppermute | solution.py:258
  481.6 2.4 multiply_subtract_fusion.1
  484.0 2.6 copy.210
  486.6 2.4 copy.211
  489.1 2.4 copy.212
  491.5 47.8 %reduce-scatter.20.cloned.1.call-done = bf16[48,2304]{1,0:T(8,128)(2,1)} async-done(((bf16[768,2304]{1,0:T(8,128)(2,1)}), bf16[48,2304]{1,0:T(8,128)(2,1)}) %reduce-scatter.20.cloned.1.call-update) | async-done | bytes 221200 | tf_op jit(solution)/shard_map/reduce_scatter | solution.py:257
  547.6 3.7 multiply_subtract_fusion
  551.2 2.5 copy.213
  553.7 2.4 copy.214
  (141 shorter events, 52.3 us)
Async XLA Ops:
  7.2 54.1 %all-gather.5.cloned.1.call-start = ((), (), s32[]{:S(2)}) async-start(), calls=%async_computation.5 | async-start | bytes 3969024 | tf_op jit(solution)/shard_map/all_gather | solution.py:254
  9.8 97.1 %all-gather.7.cloned.1.call-start = ((), (), s32[]{:S(2)}) async-start(), calls=%async_computation.6 | async-start | bytes 1253376 | tf_op jit(solution)/shard_map/all_gather | solution.py:254
  11.4 139.2 %all-gather.9.cloned.1.call-start = ((), (), s32[]{:S(2)}) async-start(), calls=%async_computation.7 | async-start | bytes 3760128 | tf_op jit(solution)/shard_map/all_gather | solution.py:254
  13.2 179.4 %all-gather.11.cloned.1.call-start = ((), (), s32[]{:S(2)}) async-start(), calls=%async_computation.8 | async-start | bytes 1880064 | tf_op jit(solution)/shard_map/all_gather | solution.py:254
  14.9 330.7 %reduce-scatter.12.cloned.1.call-start = ((), (), s32[]{:S(2)}) async-start(), calls=%async_computation.9 | async-start | bytes 1253376 | tf_op jit(solution)/shard_map/reduce_scatter | solution.py:257
  19.4 5.5 copy-start.8
  20.5 281.5 %copy-start.23 = (f32[1536]{0:T(1024)}, f32[1536]{0:T(1024)S(1)}, u32[]{:S(2)}) copy-start(f32[1536]{0:T(1024)S(1)} %add_rsqrt_fusion.1) | copy-start | bytes 18436
  62.6 152.3 %copy-start.27 = (f32[768]{0:T(1024)}, f32[768]{0:T(1024)S(1)}, u32[]{:S(2)}) copy-start(f32[768]{0:T(1024)S(1)} %get-tuple-element.146) | copy-start | bytes 9220
  62.6 239.4 %copy-start.26 = (f32[768]{0:T(1024)}, f32[768]{0:T(1024)S(1)}, u32[]{:S(2)}) copy-start(f32[768]{0:T(1024)S(1)} %get-tuple-element.147) | copy-start | bytes 9220
  102.6 2.8 copy-start
  105.5 1.5 copy-start.6
  111.8 2.2 copy-start.13
  114.6 100.3 %copy-start.25 = (f32[1536]{0:T(1024)}, f32[1536]{0:T(1024)S(1)}, u32[]{:S(2)}) copy-start(f32[1536]{0:T(1024)S(1)} %add_rsqrt_fusion) | copy-start | bytes 18436
  192.6 13.0 %copy-start.14 = (f32[1536,768]{0,1:T(8,128)S(1)}, f32[1536,768]{0,1:T(8,128)}, u32[]{:S(2)}) copy-start(f32[1536,768]{0,1:T(8,128)} %copy-done.13) | copy-start | bytes 14155780
  192.6 13.0 %copy-start.31 = (bf16[768,2304]{1,0:T(8,128)(2,1)S(1)}, bf16[768,2304]{1,0:T(8,128)(2,1)}, u32[]{:S(2)}) copy-start(bf16[768,2304]{1,0:T(8,128)(2,1)} %all-gather.9.cloned.1.call-done) | copy-start | bytes 10616836
  205.6 9.3 %copy-start.15 = (bf16[1536,768]{0,1:T(8,128)(2,1)S(1)}, bf16[1536,768]{0,1:T(8,128)(2,1)}, u32[]{:S(2)}) copy-start(bf16[1536,768]{0,1:T(8,128)(2,1)} %copy.191) | copy-start | bytes 7077892
  214.9 3.8 copy-start.7
  216.6 2.1 copy-start.12
  221.9 141.3 %reduce-scatter.14.cloned.1.call-start = ((), (), s32[]{:S(2)}) async-start(), calls=%async_computation.10 | async-start | bytes 1880064 | tf_op jit(solution)/shard_map/reduce_scatter | solution.py:257
  229.0 175.6 %reduce-scatter.16.cloned.1.call-start = ((), (), s32[]{:S(2)}) async-start(), calls=%async_computation.11 | async-start | bytes 1880064
  233.9 24.9 %copy-start.1 = (bf16[1536,768]{1,0:T(8,128)(2,1)}, bf16[1536,768]{1,0:T(8,128)(2,1)S(1)}, u32[]{:S(2)}) copy-start(bf16[1536,768]{1,0:T(8,128)(2,1)S(1)} %convolution_convert_fusion.4.dctx_ref) | copy-start | bytes 7077892
  233.9 26.6 %copy-start.9 = (bf16[1536,768]{0,1:T(8,128)(2,1)S(1)}, bf16[1536,768]{0,1:T(8,128)(2,1)}, u32[]{:S(2)}) copy-start(bf16[1536,768]{0,1:T(8,128)(2,1)} %copy-done.8) | copy-start | bytes 7077892
  258.7 1.8 copy-start.4
  265.1 203.3 %reduce-scatter.18.cloned.1.call-start = ((), (), s32[]{:S(2)}) async-start(), calls=%async_computation.12 | async-start | bytes 2088960
  265.1 3.2 copy-start.5
  268.3 3.2 copy-start.2
  271.6 24.1 %copy-start.10 = (bf16[1536,768]{0,1:T(8,128)(2,1)S(1)}, bf16[1536,768]{0,1:T(8,128)(2,1)}, u32[]{:S(2)}) copy-start(bf16[1536,768]{0,1:T(8,128)(2,1)} %copy-done.8) | copy-start | bytes 7077892
  295.6 6.2 %copy-start.3 = (bf16[1536,1152]{1,0:T(8,128)(2,1)}, bf16[1536,1152]{1,0:T(8,128)(2,1)S(1)}, u32[]{:S(2)}) copy-start(bf16[1536,1152]{1,0:T(8,128)(2,1)S(1)} %shard_map.307) | copy-start | bytes 10616836
  295.6 6.4 %copy-start.11 = (bf16[1536,768]{0,1:T(8,128)(2,1)S(1)}, bf16[1536,768]{0,1:T(8,128)(2,1)}, u32[]{:S(2)}) copy-start(bf16[1536,768]{0,1:T(8,128)(2,1)} %copy-done.8) | copy-start | bytes 7077892
  308.9 230.4 %reduce-scatter.20.cloned.1.call-start = ((), (), s32[]{:S(2)}) async-start(), calls=%async_computation.13 | async-start | bytes 3760128 | tf_op jit(solution)/shard_map/reduce_scatter | solution.py:257
  337.3 0.7 copy-start.24
  345.6 18.1 %collective-permute-start.2 = (bf16[48,768]{1,0:T(8,128)(2,1)}, bf16[48,768]{1,0:T(8,128)(2,1)}, u32[]{:S(2)}, u32[]{:S(2)}) collective-permute-start(bf16[48,768]{1,0:T(8,128)(2,1)} %reduce-scatter.12.cloned.1.call-done), channel_id=1, source_target_pairs={{0,1},{1,0},{2,3},{3,2},{4,5},{5,4},{6,7},{7,6},{8,9},{9,8},{10,11... | collective-permute-start | bytes 221192 | tf_op jit(solution)/shard_map/ppermute | solution.py:258
  363.2 44.7 %collective-permute-start.4 = (bf16[72,768]{1,0:T(8,128)(2,1)}, bf16[72,768]{1,0:T(8,128)(2,1)}, u32[]{:S(2)}, u32[]{:S(2)}) collective-permute-start(bf16[72,768]{1,0:T(8,128)(2,1)} %reduce-scatter.14.cloned.1.call-done), channel_id=1, source_target_pairs={{0,1},{1,0},{2,3},{3,2},{4,5},{5,4},{6,7},{7,6},{8,9},{9,8},{10,11... | collective-permute-start | bytes 331784 | tf_op jit(solution)/shard_map/ppermute | solution.py:258
  365.7 115.9 %copy-start.18 = (f32[48,2304]{0,1:T(8,128)S(1)}, f32[48,2304]{0,1:T(8,128)}, u32[]{:S(2)}) copy-start(f32[48,2304]{0,1:T(8,128)} %copy.200) | copy-start | bytes 1327108
  365.7 115.9 %copy-start.19 = (f32[48,2304]{0,1:T(8,128)S(1)}, f32[48,2304]{0,1:T(8,128)}, u32[]{:S(2)}) copy-start(f32[48,2304]{0,1:T(8,128)} %copy.194) | copy-start | bytes 1327108
  406.4 7.4 %collective-permute-start = (bf16[48,1152]{0,1:T(8,128)(2,1)}, bf16[48,1152]{0,1:T(8,128)(2,1)S(1)}, u32[]{:S(2)}, u32[]{:S(2)}) collective-permute-start(bf16[48,1152]{0,1:T(8,128)(2,1)} %copy.219), channel_id=1, source_target_pairs={{0,1},{1,0},{2,3},{3,2},{4,5},{5,4},{6,7},{7,6},{8,9},{9,8},{10,11... | collective-permute-start | bytes 331784 | tf_op jit(solution)/shard_map/ppermute | solution.py:258
  470.2 11.4 %copy-start.20 = (f32[48,2304]{0,1:T(8,128)S(1)}, f32[48,2304]{0,1:T(8,128)}, u32[]{:S(2)}) copy-start(f32[48,2304]{0,1:T(8,128)} %copy.198) | copy-start | bytes 1327108
  470.2 8.1 %collective-permute-start.1 = (bf16[48,1280]{0,1:T(8,128)(2,1)}, bf16[48,1280]{0,1:T(8,128)(2,1)S(1)}, u32[]{:S(2)}, u32[]{:S(2)}) collective-permute-start(bf16[48,1280]{0,1:T(8,128)(2,1)} %copy.221), channel_id=1, source_target_pairs={{0,1},{1,0},{2,3},{3,2},{4,5},{5,4},{6,7},{7,6},{8,9},{9,8},{10,11... | collective-permute-start | bytes 368648 | tf_op jit(solution)/shard_map/ppermute | solution.py:258
  479.4 2.2 copy-start.22
  484.0 56.8 %copy-start.28 = (f32[48,2]{0,1:T(2,128)S(1)}, f32[48,2]{0,1:T(2,128)}, u32[]{:S(2)}) copy-start(f32[48,2]{0,1:T(2,128)} %param.25) | copy-start | bytes 1156
  484.0 56.8 %copy-start.29 = (f32[48,2]{0,1:T(2,128)S(1)}, f32[48,2]{0,1:T(2,128)}, u32[]{:S(2)}) copy-start(f32[48,2]{0,1:T(2,128)} %param.34) | copy-start | bytes 1156
  484.0 56.8 %copy-start.30 = (f32[48,2]{0,1:T(2,128)S(1)}, f32[48,2]{0,1:T(2,128)}, u32[]{:S(2)}) copy-start(f32[48,2]{0,1:T(2,128)} %param.35) | copy-start | bytes 1156
  484.0 63.6 %copy-start.16 = (f32[48,2304]{0,1:T(8,128)S(1)}, f32[48,2304]{0,1:T(8,128)}, u32[]{:S(2)}) copy-start(f32[48,2304]{0,1:T(8,128)} %copy.201) | copy-start | bytes 1327108
  484.0 63.6 %copy-start.17 = (f32[48,2304]{0,1:T(8,128)S(1)}, f32[48,2304]{0,1:T(8,128)}, u32[]{:S(2)}) copy-start(f32[48,2304]{0,1:T(8,128)} %copy.205) | copy-start | bytes 1327108
  539.3 6.2 %collective-permute-start.3 = (bf16[48,2304]{1,0:T(8,128)(2,1)}, bf16[48,2304]{1,0:T(8,128)(2,1)}, u32[]{:S(2)}, u32[]{:S(2)}) collective-permute-start(bf16[48,2304]{1,0:T(8,128)(2,1)} %reduce-scatter.20.cloned.1.call-done), channel_id=1, source_target_pairs={{0,1},{1,0},{2,3},{3,2},{4,5},{5,4},{6,7},{7,6},{8,9},{9,8},{10,11... | collective-permute-start | bytes 663560 | tf_op jit(solution)/shard_map/ppermute | solution.py:258
  551.2 4.9 copy-start.21
Sparse Core Ops, SparseCore 0:
  10.8 50.5 all-gather.4
  64.2 37.3 all-gather.6
  104.5 46.1 all-gather.8
  153.2 39.3 all-gather.10
  222.0 56.6 reduce-scatter.11
  282.4 59.2 reduce-scatter.13
  345.5 59.0 reduce-scatter.15
  408.3 60.0 reduce-scatter.17
  472.3 67.0 reduce-scatter.19

commit v2 on v1

--- a/solution.py
+++ b/solution.py
@@ -5,6 +5,7 @@
 import jax.numpy as jnp
 from jax import lax
 from jax.experimental import pallas as pl
+from jax.experimental.layout import Layout, with_layout_constraint
 from jax.experimental.pallas import tpu as pltpu
 from jax.sharding import PartitionSpec as P
 
@@ -20,6 +21,10 @@
 decay_rate = 1e-05
 inv_root_two = 0.7071067811865476
 inv_root_tau = 0.3989422804014327
+
+
+def row_major(values):
+    return with_layout_constraint(values, Layout(major_to_minor=(0, 1)))
 
 
 def normalize(values):
@@ -253,19 +258,51 @@
     def gather(value):
         return lax.all_gather(value, "dp", axis=0, tiled=True)
 
-    def reduce_owned(value):
-        part = lax.psum_scatter(value, "dp", scatter_dimension=0, tiled=True)
+    def scatter(value):
+        return lax.psum_scatter(value, "dp", scatter_dimension=0, tiled=True)
+
+    def both_replicas(part):
         other = lax.ppermute(part, "rep", [(i, rep_size - 1 - i) for i in range(rep_size)])
-        return part.astype(jnp.float32) + other.astype(jnp.float32)
-
-    padded_gains = jnp.pad(norm_gains, ((0, 0), (0, 126)))
-    packed = gather(jnp.concatenate([qkv_weight, padded_gains], 1).astype(jnp.bfloat16))
-    w_attn = gather(attn_out_weight.astype(jnp.bfloat16))
-    w_in = gather(mlp_in_weight.astype(jnp.bfloat16))
-    w_out = gather(mlp_out_weight.astype(jnp.bfloat16))
+        return row_major(part.astype(jnp.float32) + other.astype(jnp.float32))
+
+    owners = width // qkv_weight.shape[0]
+    own = qkv_weight.shape[0]
+    rest = mlp_out_weight.shape[0] - own
+    fold = own // rest
+
+    def fold_rows(value):
+        blocks = value.reshape(-1, own + rest, width)
+        head = blocks[:, :own].reshape(-1, width)
+        tail = blocks[:, own:]
+        piece = width // fold
+        tail = jnp.concatenate([tail[:, :, n * piece : (n + 1) * piece] for n in range(fold)], 1)
+        return head, tail.reshape(-1, piece)
+
+    def unfold_rows(head, tail):
+        piece = width // fold
+        blocks = tail.reshape(-1, own, piece)
+        tail = jnp.concatenate([blocks[:, n * rest : (n + 1) * rest] for n in range(fold)], 2)
+        return jnp.concatenate([head.reshape(-1, own, width), tail], 1).reshape(-1, width)
+
+    padded_gains = row_major(jnp.pad(norm_gains, ((0, 0), (0, 126))).astype(jnp.bfloat16))
+    packed = gather(jnp.concatenate([qkv_weight.astype(jnp.bfloat16), padded_gains], 1))
     w_qkv = packed[:, : 3 * width]
     gain_one = packed[:, 3 * width].astype(jnp.float32)
     gain_two = packed[:, 3 * width + 1].astype(jnp.float32)
+    others = gather(
+        jnp.concatenate(
+            [
+                mlp_in_weight.astype(jnp.bfloat16),
+                attn_out_weight.astype(jnp.bfloat16),
+                *fold_rows(mlp_out_weight.astype(jnp.bfloat16)),
+            ],
+            1,
+        )
+    )
+    at_a, at_o = 2 * ff_width, 2 * ff_width + width
+    w_in = others[:, :at_a]
+    w_attn = others[:, at_a:at_o]
+    w_out = unfold_rows(others[:, at_o : at_o + width], others[:, at_o + width :])
 
     seg_ids, positions = segments(lengths, rows)
     cos_tab, sin_tab = rope_tables(positions.reshape(-1))
@@ -276,7 +313,7 @@
     h_one = (hat_one * gain_one).astype(jnp.bfloat16)
     qkv_all = jnp.dot(h_one, w_qkv, preferred_element_type=jnp.float32)
     rot, context = attn_forward(qkv_all, cos_tab, sin_tab, seg_col, micro)
-    middle = x_float + jnp.dot(context, w_attn, preferred_element_type=jnp.float32)
+    middle = row_major(x_float + jnp.dot(context, w_attn, preferred_element_type=jnp.float32))
     hat_two, inv_two = normalize(middle)
     h_two = (hat_two * gain_two).astype(jnp.bfloat16)
     gate_up = jnp.dot(h_two, w_in, preferred_element_type=jnp.float32)
@@ -289,7 +326,6 @@
     grad_float = cotangent.astype(jnp.float32)
     grad_hidden = contract_cols(cotangent, w_out)
     grad_wo = contract_rows(hidden, cotangent).astype(jnp.bfloat16)
-    sum_o = reduce_owned(grad_wo)
     activations = (middle + jnp.dot(hidden, w_out, preferred_element_type=jnp.float32)).astype(
         jnp.bfloat16
     )
@@ -298,45 +334,33 @@
     )
     grad_gate = grad_hidden * act_out
     grad_gu = jnp.concatenate([grad_act, grad_gate], 1).astype(jnp.bfloat16)
-    sum_i = reduce_owned(contract_rows(h_two, grad_gu).astype(jnp.bfloat16))
-    grad_h_two = contract_cols(grad_gu, w_in)
+    grad_wi = contract_rows(h_two, grad_gu).astype(jnp.bfloat16)
+    grad_h_two = row_major(contract_cols(grad_gu, w_in))
     grad_mid = grad_float + norm_back(grad_h_two, hat_two, inv_two, gain_two)
     grad_g_two = jnp.sum(grad_h_two * hat_two, 0)
     grad_mid_low = grad_mid.astype(jnp.bfloat16)
-    sum_a = reduce_owned(contract_rows(context, grad_mid_low).astype(jnp.bfloat16))
+    grad_wa = contract_rows(context, grad_mid_low).astype(jnp.bfloat16)
+    early = jnp.concatenate([grad_wi, grad_wa, *fold_rows(grad_wo)], 1)
     grad_ctx = contract_cols(grad_mid_low, w_attn).astype(jnp.bfloat16)
-
-    half = PAIRS // 2
-    side = half * PAIR
-    grads_qkv, sums_q = [], []
-    grad_h_one = None
-    for part in range(2):
-        grad_qkv = attn_backward(
-            rot, grad_ctx, cos_tab, sin_tab, seg_col, micro, part * half, half
-        )
-        w_part = jnp.concatenate(
-            [
-                w_qkv[:, n * width + part * side : n * width + (part + 1) * side]
-                for n in range(3)
-            ],
-            1,
-        )
-        term = contract_cols(grad_qkv, w_part)
-        grad_h_one = term if grad_h_one is None else grad_h_one + term
-        grad_wq = contract_rows(h_one, grad_qkv).astype(jnp.bfloat16)
-        if part == 0:
-            sums_q.append(reduce_owned(grad_wq))
+    early, grad_ctx = lax.optimization_barrier((early, grad_ctx))
+    early = scatter(early)
+    grad_qkv = attn_backward(rot, grad_ctx, cos_tab, sin_tab, seg_col, micro, 0, PAIRS)
+    grad_h_one = row_major(contract_cols(grad_qkv, w_qkv))
+    grad_wq = contract_rows(h_one, grad_qkv).astype(jnp.bfloat16)
     grad_g_one = jnp.sum(grad_h_one * hat_one, 0)
     grad_gains = jnp.stack([grad_g_one, grad_g_two], 1).astype(jnp.bfloat16)
-    tail = reduce_owned(
-        jnp.concatenate([grad_wq, jnp.pad(grad_gains, ((0, 0), (0, 126)))], 1)
-    )
-    sums_q.append(tail[:, : 3 * side])
-    sum_g = tail[:, 3 * side : 3 * side + 2]
+    grad_gains = row_major(jnp.pad(grad_gains, ((0, 0), (0, 126))))
+    last = jnp.concatenate([grad_wq, grad_gains], 1)
+    early, last = lax.optimization_barrier((early, last))
+    last = both_replicas(scatter(last))
+    early = both_replicas(early)
+    sum_i = early[:, :at_a]
+    sum_a = early[:, at_a:at_o]
+    sum_o = unfold_rows(early[:, at_o : at_o + width], early[:, at_o + width :])
+
+    sum_q = last[:, : 3 * width]
+    sum_g = last[:, 3 * width : 3 * width + 2]
     input_grad = grad_mid + norm_back(grad_h_one, hat_one, inv_one, gain_one)
-    sum_q = jnp.concatenate(
-        [sums_q[part][:, n * side : (n + 1) * side] for n in range(3) for part in range(2)], 1
-    )
 
     qkv_res = adam_update(qkv_weight, qkv_first, qkv_second, sum_q, 0.03)
     attn_res = adam_update(attn_out_weight, attn_first, attn_second, sum_a, 0.3)

time: 574 us -> 378 us (0.66)
  waiting for transfers between devices: 249 us -> 138 us
  local copies, waits for them, and re-layouts: 68.4 us -> 14.2 us
  matrix products: 104 us -> 92.5 us
  other arithmetic: 43.9 us -> 36.1 us
    unnamed x11 -> x4, waiting for transfers between devices: 91.8 us -> 0.07 us
    unnamed x89 -> x70, local copies, waits for them, and re-layouts: 63.4 us -> 11 us
    all_gather x4 -> x2, waiting for transfers between devices: 98.5 us -> 59.6 us  [gather(): return lax.all_gather(value, 'dp', axis=0, tiled=True)]
    reduce_scatter x3 -> x2, waiting for transfers between devices: 47.8 us -> 71.1 us  [scatter(): return lax.psum_scatter(value, 'dp', scatter_dimension=0, tiled=True)]
    dot_general x5 -> x4, matrix products: 32.1 us -> 23.7 us  [contract_rows(): lax.dot_general(left, right, (((0,), (0,)), ((), ())), preferred_element_...]
    sub x5, other arithmetic: 11.5 us -> 4.35 us  [adam_update(): weight - rate * (direction + decay_rate * weight)]
    pallas_call x2 -> x1, Pallas kernels: 48.8 us -> 46.6 us  [attn_backward(): pl.pallas_call(attn_bwd_kernel, grid=(micro, count), in_specs=[pl.BlockSp...]
    dot_general x5 -> x4, matrix products: 36.5 us -> 36.4 us  [contract_cols(): lax.dot_general(left, right, (((1,), (1,)), ((), ())), preferred_element_...]
  transfers between devices with their start and end apart: 14 -> 6, of which waited for: 9 -> 6; matrix products, arithmetic and copies ran while one was open for 29% -> 16% of each run, Pallas kernels for 14% -> 20%
where the time goes in v2:
time: 378 us; the launch traced here: 373 us
  waiting for transfers between devices  138 us (37%)
  matrix products  92.5 us (24%)
  Pallas kernels  74.6 us (20%)
  other arithmetic  36.1 us (10%)
  between operations  14.6 us (4%)
  local copies, waits for them, and re-layouts  14.2 us (4%)
    reduce_scatter x2, waiting for transfers between devices, scatter(): return lax.psum_scatter(value, 'dp', scatter_dimension=0, tiled=True)  71.1 us
    all_gather x2, waiting for transfers between devices, gather(): return lax.all_gather(value, 'dp', axis=0, tiled=True)  59.6 us
    pallas_call x1, Pallas kernels, attn_backward(): pl.pallas_call(attn_bwd_kernel, grid=(micro, count), in_specs=[pl.BlockSp...  46.6 us
    dot_general x4, matrix products, contract_cols(): lax.dot_general(left, right, (((1,), (1,)), ((), ())), preferred_element_...  36.4 us
    pallas_call x1, Pallas kernels, attn_forward(): pl.pallas_call(attn_fwd_kernel, grid=(micro, PAIRS), in_specs=[pl.BlockSp...  28 us
    dot_general x4, matrix products, contract_rows(): lax.dot_general(left, right, (((0,), (0,)), ((), ())), preferred_element_...  23.7 us
    dot_general x1, matrix products, local(): qkv_all = jnp.dot(h_one, w_qkv, preferred_element_type=jnp.float32)  11.8 us
    unnamed x70, local copies, waits for them, and re-layouts  11 us
  transfers between devices with their start and end apart: 6, of which 6 were waited for; matrix products, arithmetic and copies ran while one was open for 16% of the time, Pallas kernels for 20%

profile of v2, /device:TPU:0, one launch (start us, length us, event | category | flops | bytes accessed | tf_op | source)
XLA Modules:
  0.0 373.1 jit_solution(12091135902288726113)
XLA Ops:
  7.2 1.2 convert_element_type.108
  9.2 0.7 fusion.36
  10.0 1.0 convert_element_type.116
  11.1 0.9 convert_element_type.117
  12.0 1.0 convert_bitcast_fusion
  13.0 0.8 pad_maximum_fusion.7
  13.8 0.9 reduce_window_sum.11
  16.0 0.8 fusion.18
  16.9 2.8 fusion.35
  19.7 1.3 pad_maximum_fusion.4
  21.0 40.4 %all-gather.3.cloned.1.call-done = bf16[768,2432]{1,0:T(8,128)(2,1)} async-done(((bf16[48,2432]{1,0:T(8,128)(2,1)}), bf16[768,2432]{1,0:T(8,128)(2,1)}) %all-gather.3.cloned.1.call-update) | async-done | bytes 3735568 | tf_op jit(solution)/shard_map/all_gather | solution.py:259
  61.4 1.3 convert_reduce_fusion.1
  62.6 11.8 %fusion.26.q_ref.k_ref.v_ref = f32[1536,2304]{1,0:T(8,128)} fusion(bf16[768,2432]{1,0:T(8,128)(2,1)} %all-gather.3.cloned.1.call-done, bf16[1536,768]{1,0:T(8,128)(2,1)} %param.18, f32[768]{0:T(1024)S(1)} %get-tuple-element.121, f32[1536]{0:T(1024)S(1)} %add_rsqrt_fusion.1, f32[1536]{0:T(1024)S(1)} %broadcast_multiply_fusion.6), kind=kOutput, calls=%fused_computation.51 | convolution fusion | flops 5441716224 | bytes 20069376 | tf_op jit(solution)/shard_map/dot_general | solution.py:314
  74.7 28.0 %shard_map.305 = (bf16[1536,2304]{1,0:T(8,128)(2,1)S(1)}, bf16[1536,768]{1,0:T(8,128)(2,1)S(1)}) custom-call(f32[1536,2304]{1,0:T(8,128)} %fusion.26.q_ref.k_ref.v_ref, f32[1536,2304]{1,0:T(8,128)} %fusion.26.q_ref.k_ref.v_ref, f32[1536,2304]{1,0:T(8,128)} %fusion.26.q_ref.k_ref.v_ref, f32[1536,128]{1,0:T(8,128)S(1)} %get-tuple-element.159.cos_ref, ...), custom_call_target="tpu_custom_call" | custom-call | flops 4831838208 | bytes 24772608 | tf_op jit(solution)/shard_map/pallas_call | solution.py:169
  102.8 2.8 copy-done
  105.6 1.4 copy-done.1
  107.0 19.2 %all-gather.5.cloned.1.call-done = bf16[768,4224]{1,0:T(8,128)(2,1)} async-done(((bf16[48,4224]{1,0:T(8,128)(2,1)}), bf16[768,4224]{1,0:T(8,128)(2,1)}) %all-gather.5.cloned.1.call-update) | async-done | bytes 6488080 | tf_op jit(solution)/shard_map/all_gather | solution.py:259
  126.2 5.0 %fusion.53 = (f32[1536]{0:T(1024)S(1)}, f32[1536,768]{1,0:T(8,128)S(1)}) fusion(bf16[1536,768]{1,0:T(8,128)(2,1)} %copy-done.1, bf16[768,4224]{1,0:T(8,128)(2,1)} %all-gather.5.cloned.1.call-done, bf16[1536,768]{1,0:T(8,128)(2,1)} %param.18), kind=kOutput, calls=%fused_computation.124 | convolution fusion | flops 1815476736 | bytes 10622976 | tf_op jit(solution)/shard_map/dot_general | solution.py:316
  131.9 0.7 slice-done
  132.7 1.2 slice-done.1
  134.1 2.9 copy-done.10
  137.0 9.3 %fusion.22 = f32[1536,2304]{1,0:T(8,128)} fusion(bf16[768,4224]{1,0:T(8,128)(2,1)S(1)} %copy-done.10, f32[1536,768]{1,0:T(8,128)S(1)} %get-tuple-element.156, f32[768]{0:T(1024)S(1)} %get-tuple-element.120, f32[1536]{0:T(1024)S(1)} %add_rsqrt_fusion, f32[1536]{0:T(1024)S(1)} %broadcast_multiply_fusion.5), kind=kOutput, calls=%fused_computation.47 | convolution fusion | flops 5440536576 | bytes 22433792 | tf_op jit(solution)/shard_map/dot_general | solution.py:319
  146.3 12.0 %fusion.5 = (bf16[1536,1152]{1,0:T(8,128)(2,1)}, bf16[1536,1152]{1,0:T(8,128)(2,1)}, bf16[1536,1152]{1,0:T(8,128)(2,1)S(1)}) fusion(f32[1536,2304]{1,0:T(8,128)} %fusion.22, bf16[1152,768]{1,0:T(8,128)(2,1)S(1)} %bitcast.40, bf16[1536,768]{1,0:T(8,128)(2,1)S(1)} %copy-done.11), kind=kOutput, calls=%fused_computation.8 | convolution fusion | flops 2746220544 | bytes 28901376 | tf_op jit(solution)/shard_map/dot_general | solution.py:73
  158.3 3.1 convolution_convert_fusion.3
  161.6 9.2 %convolution_convert_fusion.1 = bf16[768,2304]{1,0:T(8,128)(2,1)S(1)} fusion(bf16[1536,1152]{1,0:T(8,128)(2,1)} %get-tuple-element.139, bf16[1536,1152]{1,0:T(8,128)(2,1)} %get-tuple-element.138, f32[1536,768]{1,0:T(8,128)S(1)} %get-tuple-element.156, f32[768]{0:T(1024)S(1)} %get-tuple-element.120, f32[1536]{0:T(1024)S(1)} %add_rsqrt_fusion, ...), kind=kOutput, calls=%fused_computation.25 | convolution fusion | flops 5456461824 | bytes 15350784 | tf_op jit(solution)/shard_map/dot_general | solution.py:67
  170.8 10.1 %multiply_reduce_fusion = (bf16[768]{0:T(1024)(128)(2,1)S(1)}, f32[1536]{0:T(1024)S(1)}, f32[1536]{0:T(1024)S(1)}, f32[1536,768]{1,0:T(8,128)S(1)}) fusion(f32[1536,768]{1,0:T(8,128)S(1)} %get-tuple-element.156, f32[1536]{0:T(1024)S(1)} %add_rsqrt_fusion, f32[1536]{0:T(1024)S(1)} %broadcast_multiply_fusion.5, f32[768]{0:T(1024)S(1)} %get-tuple-element.120, ...), kind=kOutput, calls=%fused_computation.33 | convolution fusion | flops 5459406848 | bytes 20083200 | tf_op jit(solution)/shard_map/dot_general | solution.py:73
  181.0 3.7 multiply_add_fusion
  184.8 2.1 convolution_convert_fusion.4
  187.0 3.2 pad_maximum_fusion.1
  190.2 6.1 %convolution_convert_fusion.2.dctx_ref = bf16[1536,768]{1,0:T(8,128)(2,1)} fusion(f32[1536,768]{1,0:T(8,128)} %copy-done.8, bf16[768,4224]{1,0:T(8,128)(2,1)} %all-gather.5.cloned.1.call-done), kind=kOutput, calls=%fused_computation.44 | convolution fusion | flops 1814298624 | bytes 8257536 | tf_op jit(solution)/shard_map/dot_general | solution.py:73
  196.4 1.7 copy-done.4
  198.1 46.6 %shard_map.306 = bf16[1536,2304]{1,0:T(8,128)(2,1)S(1)} custom-call(bf16[1536,2304]{1,0:T(8,128)(2,1)} %copy-done, bf16[1536,2304]{1,0:T(8,128)(2,1)} %copy-done, bf16[1536,2304]{1,0:T(8,128)(2,1)} %copy-done, bf16[1536,768]{1,0:T(8,128)(2,1)S(1)} %copy-done.4, f32[1536,128]{1,0:T(8,128)S(1)} %get-tuple-element.159.cos_ref, ...), custom_call_target="tpu_custom_call" | custom-call | flops 12079595520 | bytes 16515072 | tf_op jit(solution)/shard_map/pallas_call | solution.py:200
  244.8 8.0 %fusion.17 = (bf16[768]{0:T(1024)(128)(2,1)S(1)}, f32[1536]{0:T(1024)S(1)}, f32[1536]{0:T(1024)S(1)}, f32[1536,768]{1,0:T(8,128)}) fusion(bf16[1536,768]{1,0:T(8,128)(2,1)S(1)} %copy-done.6, f32[1536]{0:T(1024)S(1)} %add_rsqrt_fusion.1, f32[1536]{0:T(1024)S(1)} %broadcast_multiply_fusion.6, f32[768]{0:T(1024)S(1)} %get-tuple-element.121, ...), kind=kOutput, calls=%fused_computation.31 | convolution fusion | flops 5446430720 | bytes 17729024 | tf_op jit(solution)/shard_map/dot_general | solution.py:73
  253.0 9.4 %convolution_convert_fusion = bf16[768,2304]{1,0:T(8,128)(2,1)S(1)} fusion(bf16[1536,2304]{1,0:T(8,128)(2,1)} %copy-done.3, bf16[1536,768]{1,0:T(8,128)(2,1)S(1)} %copy-done.7, f32[768]{0:T(1024)S(1)} %get-tuple-element.121, f32[1536]{0:T(1024)S(1)} %add_rsqrt_fusion.1, f32[1536]{0:T(1024)S(1)} %broadcast_multiply_fusion.6), kind=kOutput, calls=%fused_computation.24 | convolution fusion | flops 5443485696 | bytes 12991488 | tf_op jit(solution)/shard_map/dot_general | solution.py:67
  262.5 2.1 fusion.20
  264.5 17.7 %reduce-scatter.3.cloned.1.call-done = bf16[48,4224]{1,0:T(8,128)(2,1)} async-done(((bf16[768,4224]{1,0:T(8,128)(2,1)}), bf16[48,4224]{1,0:T(8,128)(2,1)}) %reduce-scatter.3.cloned.1.call-update) | async-done | bytes 405520 | tf_op jit(solution)/shard_map/reduce_scatter | solution.py:262
  282.6 6.1 %fusion.16 = f32[1536,768]{1,0:T(8,128)} fusion(f32[1536,768]{1,0:T(8,128)} %copy-done.8, bf16[1536,768]{1,0:T(8,128)(2,1)S(1)} %copy-done.7, f32[1536,768]{1,0:T(8,128)} %get-tuple-element.158, f32[1536]{0:T(1024)S(1)} %broadcast_multiply_fusion.1, f32[1536]{0:T(1024)S(1)} %broadcast_multiply_fusion.2, f32[768]{0:T(1024)S(1)} %get-tuple-element.121, ...), kind=kLoop, calls=%fused_computation.30 | loop fusion | flops 10616832 | bytes 16542720 | tf_op jit(solution)/shard_map/add | solution.py:363
  288.8 1.5 collective-permute-start.1
  290.3 6.2 %add_convert_fusion = bf16[1536,768]{1,0:T(8,128)(2,1)} fusion(f32[1536,768]{1,0:T(8,128)} %copy-done.9, bf16[1536,1152]{1,0:T(8,128)(2,1)S(1)} %copy-done.32, bf16[1152,768]{1,0:T(8,128)(2,1)S(1)} %bitcast.41), kind=kOutput, calls=%fused_computation.36 | convolution fusion | flops 2720268288 | bytes 12386304 | tf_op jit(solution)/shard_map/dot_general | solution.py:329
  296.6 3.3 collective-permute-done.1
  300.1 0.8 multiply_subtract_fusion.3
  300.9 1.3 multiply_subtract_fusion
  302.2 53.4 %reduce-scatter.5.cloned.1.call-done = bf16[48,2432]{1,0:T(8,128)(2,1)} async-done(((bf16[768,2432]{1,0:T(8,128)(2,1)}), bf16[48,2432]{1,0:T(8,128)(2,1)}) %reduce-scatter.5.cloned.1.call-update) | async-done | bytes 233488 | tf_op jit(solution)/shard_map/reduce_scatter | solution.py:262
  355.6 1.4 collective-permute-start
  357.0 0.9 multiply_subtract_fusion.2
  358.0 3.9 %collective-permute-done = bf16[48,2432]{1,0:T(8,128)(2,1)S(1)} collective-permute-done((bf16[48,2432]{1,0:T(8,128)(2,1)}, bf16[48,2432]{1,0:T(8,128)(2,1)S(1)}, u32[]{:S(2)}, u32[]{:S(2)}) %collective-permute-start) | collective-permute-done | bytes 233504 | tf_op jit(solution)/shard_map/ppermute | solution.py:265
  361.9 1.0 convert_add_fusion.2
  365.1 1.3 multiply_subtract_fusion.1
  (121 shorter events, 6.8 us)
Async XLA Ops:
  7.2 8.4 %copy-start.5 = (bf16[1536,768]{1,0:T(8,128)(2,1)S(1)}, bf16[1536,768]{1,0:T(8,128)(2,1)}, u32[]{:S(2)}) copy-start(bf16[1536,768]{1,0:T(8,128)(2,1)} %param.18) | copy-start | bytes 7077892
  7.2 54.2 %all-gather.3.cloned.1.call-start = ((), (), s32[]{:S(2)}) async-start(), calls=%async_computation.2 | async-start | bytes 3969024 | tf_op jit(solution)/shard_map/all_gather | solution.py:259
  10.0 116.2 %all-gather.5.cloned.1.call-start = ((), (), s32[]{:S(2)}) async-start(), calls=%async_computation.3 | async-start | bytes 6893568 | tf_op jit(solution)/shard_map/all_gather | solution.py:259
  13.8 268.4 %reduce-scatter.3.cloned.1.call-start = ((), (), s32[]{:S(2)}) async-start(), calls=%async_computation.4 | async-start | bytes 6893568 | tf_op jit(solution)/shard_map/reduce_scatter | solution.py:262
  102.8 2.8 copy-start
  105.6 1.4 copy-start.1
  131.2 49.8 %copy-start.9 = (f32[1536,768]{1,0:T(8,128)}, f32[1536,768]{1,0:T(8,128)S(1)}, u32[]{:S(2)}) copy-start(f32[1536,768]{1,0:T(8,128)S(1)} %get-tuple-element.156) | copy-start | bytes 14155780
  131.2 1.5 slice-start
  131.2 2.8 slice-start.1
  131.9 5.1 %copy-start.10 = (bf16[768,4224]{1,0:T(8,128)(2,1)S(1)}, bf16[768,4224]{1,0:T(8,128)(2,1)}, u32[]{:S(2)}) copy-start(bf16[768,4224]{1,0:T(8,128)(2,1)} %all-gather.5.cloned.1.call-done) | copy-start | bytes 19464196
  134.1 12.2 %copy-start.12 = (bf16[16,72,768]{2,1,0:T(8,128)(2,1)}, bf16[16,72,768]{2,1,0:T(8,128)(2,1)S(1)}, u32[]{:S(2)}) copy-start(bf16[16,72,768]{2,1,0:T(8,128)(2,1)S(1)} %maximum_maximum_fusion) | copy-start | bytes 5308420
  137.0 9.3 %copy-start.11 = (bf16[1536,768]{1,0:T(8,128)(2,1)S(1)}, bf16[1536,768]{1,0:T(8,128)(2,1)}, u32[]{:S(2)}) copy-start(bf16[1536,768]{1,0:T(8,128)(2,1)} %param.19) | copy-start | bytes 7077892
  158.3 3.1 copy-start.31
  181.0 3.7 %copy-start.2 = (bf16[1536,768]{1,0:T(8,128)(2,1)S(1)}, bf16[1536,768]{1,0:T(8,128)(2,1)}, u32[]{:S(2)}) copy-start(bf16[1536,768]{1,0:T(8,128)(2,1)} %copy-done.1) | copy-start | bytes 7077892
  184.8 2.2 copy-start.8
  196.4 159.2 %reduce-scatter.5.cloned.1.call-start = ((), (), s32[]{:S(2)}) async-start(), calls=%async_computation.5 | async-start | bytes 3969024 | tf_op jit(solution)/shard_map/reduce_scatter | solution.py:262
  196.4 1.7 copy-start.4
  198.1 46.6 %copy-start.6 = (bf16[1536,768]{1,0:T(8,128)(2,1)S(1)}, bf16[1536,768]{1,0:T(8,128)(2,1)}, u32[]{:S(2)}) copy-start(bf16[1536,768]{1,0:T(8,128)(2,1)} %param.18) | copy-start | bytes 7077892
  198.1 46.6 %copy-start.27 = (bf16[768,2432]{1,0:T(8,128)(2,1)S(1)}, bf16[768,2432]{1,0:T(8,128)(2,1)}, u32[]{:S(2)}) copy-start(bf16[768,2432]{1,0:T(8,128)(2,1)} %all-gather.3.cloned.1.call-done) | copy-start | bytes 11206660
  244.7 8.1 %copy-start.3 = (bf16[1536,2304]{1,0:T(8,128)(2,1)}, bf16[1536,2304]{1,0:T(8,128)(2,1)S(1)}, u32[]{:S(2)}) copy-start(bf16[1536,2304]{1,0:T(8,128)(2,1)S(1)} %shard_map.306) | copy-start | bytes 21233668
  244.7 8.3 %copy-start.7 = (bf16[1536,768]{1,0:T(8,128)(2,1)S(1)}, bf16[1536,768]{1,0:T(8,128)(2,1)}, u32[]{:S(2)}) copy-start(bf16[1536,768]{1,0:T(8,128)(2,1)} %param.18) | copy-start | bytes 7077892
  262.4 19.8 %copy-start.28 = (f32[48,2]{0,1:T(2,128)S(1)}, f32[48,2]{0,1:T(2,128)}, u32[]{:S(2)}) copy-start(f32[48,2]{0,1:T(2,128)} %param.25) | copy-start | bytes 1156
  262.4 19.9 %copy-start.29 = (f32[48,2]{0,1:T(2,128)S(1)}, f32[48,2]{0,1:T(2,128)}, u32[]{:S(2)}) copy-start(f32[48,2]{0,1:T(2,128)} %param.34) | copy-start | bytes 1156
  262.5 20.0 %copy-start.30 = (f32[48,2]{0,1:T(2,128)S(1)}, f32[48,2]{0,1:T(2,128)}, u32[]{:S(2)}) copy-start(f32[48,2]{0,1:T(2,128)} %param.35) | copy-start | bytes 1156
  282.6 6.2 %copy-start.22 = (bf16[48,4224]{1,0:T(8,128)(2,1)S(1)}, bf16[48,4224]{1,0:T(8,128)(2,1)}, u32[]{:S(2)}) copy-start(bf16[48,4224]{1,0:T(8,128)(2,1)} %reduce-scatter.3.cloned.1.call-done) | copy-start | bytes 1216516
  282.6 7.8 %copy-start.13 = (bf16[16,72,768]{2,1,0:T(8,128)(2,1)S(1)}, bf16[16,72,768]{2,1,0:T(8,128)(2,1)}, u32[]{:S(2)}) copy-start(bf16[16,72,768]{2,1,0:T(8,128)(2,1)} %copy-done.12) | copy-start | bytes 5308420
  282.6 7.7 %copy-start.32 = (bf16[1536,1152]{1,0:T(8,128)(2,1)S(1)}, bf16[1536,1152]{1,0:T(8,128)(2,1)}, u32[]{:S(2)}) copy-start(bf16[1536,1152]{1,0:T(8,128)(2,1)} %copy-done.31) | copy-start | bytes 10616836
  288.7 11.3 %copy-start.17 = (f32[48,768]{1,0:T(8,128)S(1)}, f32[48,768]{1,0:T(8,128)}, u32[]{:S(2)}) copy-start(f32[48,768]{1,0:T(8,128)} %param.22) | copy-start | bytes 442372
  288.8 11.3 %copy-start.25 = (f32[48,768]{1,0:T(8,128)S(1)}, f32[48,768]{1,0:T(8,128)}, u32[]{:S(2)}) copy-start(f32[48,768]{1,0:T(8,128)} %param.28) | copy-start | bytes 442372
  288.8 11.3 %copy-start.26 = (f32[48,768]{1,0:T(8,128)S(1)}, f32[48,768]{1,0:T(8,128)}, u32[]{:S(2)}) copy-start(f32[48,768]{1,0:T(8,128)} %param.29) | copy-start | bytes 442372
  288.8 12.2 %copy-start.14 = (f32[48,2304]{1,0:T(8,128)S(1)}, f32[48,2304]{1,0:T(8,128)}, u32[]{:S(2)}) copy-start(f32[48,2304]{1,0:T(8,128)} %param.23) | copy-start | bytes 1327108
  288.8 12.1 %copy-start.18 = (f32[48,2304]{1,0:T(8,128)S(1)}, f32[48,2304]{1,0:T(8,128)}, u32[]{:S(2)}) copy-start(f32[48,2304]{1,0:T(8,128)} %param.30) | copy-start | bytes 1327108
  288.8 12.1 %copy-start.19 = (f32[48,2304]{1,0:T(8,128)S(1)}, f32[48,2304]{1,0:T(8,128)}, u32[]{:S(2)}) copy-start(f32[48,2304]{1,0:T(8,128)} %param.31) | copy-start | bytes 1327108
  288.8 11.1 %collective-permute-start.1 = (bf16[48,4224]{1,0:T(8,128)(2,1)S(1)}, bf16[48,4224]{1,0:T(8,128)(2,1)S(1)}, u32[]{:S(2)}, u32[]{:S(2)}) collective-permute-start(bf16[48,4224]{1,0:T(8,128)(2,1)S(1)} %copy-done.22), channel_id=1, source_target_pairs={{0,1},{1,0},{2,3},{3,2},{4,5},{5,4},{6,7},{7,6},{8,9},{9,8},{10,11... | collective-permute-start | bytes 1216520 | tf_op jit(solution)/shard_map/ppermute | solution.py:265
  296.6 60.4 %copy-start.16 = (f32[72,768]{1,0:T(8,128)S(1)}, f32[72,768]{1,0:T(8,128)}, u32[]{:S(2)}) copy-start(f32[72,768]{1,0:T(8,128)} %param.24) | copy-start | bytes 663556
  296.6 60.4 %copy-start.23 = (f32[72,768]{1,0:T(8,128)S(1)}, f32[72,768]{1,0:T(8,128)}, u32[]{:S(2)}) copy-start(f32[72,768]{1,0:T(8,128)} %param.32) | copy-start | bytes 663556
  296.6 60.4 %copy-start.24 = (f32[72,768]{1,0:T(8,128)S(1)}, f32[72,768]{1,0:T(8,128)}, u32[]{:S(2)}) copy-start(f32[72,768]{1,0:T(8,128)} %param.33) | copy-start | bytes 663556
  296.6 68.5 %copy-start.15 = (f32[48,2304]{1,0:T(8,128)S(1)}, f32[48,2304]{1,0:T(8,128)}, u32[]{:S(2)}) copy-start(f32[48,2304]{1,0:T(8,128)} %param.21) | copy-start | bytes 1327108
  296.6 68.5 %copy-start.20 = (f32[48,2304]{1,0:T(8,128)S(1)}, f32[48,2304]{1,0:T(8,128)}, u32[]{:S(2)}) copy-start(f32[48,2304]{1,0:T(8,128)} %param.26) | copy-start | bytes 1327108
  296.6 68.5 %copy-start.21 = (f32[48,2304]{1,0:T(8,128)S(1)}, f32[48,2304]{1,0:T(8,128)}, u32[]{:S(2)}) copy-start(f32[48,2304]{1,0:T(8,128)} %param.27) | copy-start | bytes 1327108
  355.6 6.3 %collective-permute-start = (bf16[48,2432]{1,0:T(8,128)(2,1)}, bf16[48,2432]{1,0:T(8,128)(2,1)S(1)}, u32[]{:S(2)}, u32[]{:S(2)}) collective-permute-start(bf16[48,2432]{1,0:T(8,128)(2,1)} %reduce-scatter.5.cloned.1.call-done), channel_id=1, source_target_pairs={{0,1},{1,0},{2,3},{3,2},{4,5},{5,4},{6,7},{7,6},{8,9},{9,8},{10,11... | collective-permute-start | bytes 700424 | tf_op jit(solution)/shard_map/ppermute | solution.py:265
Sparse Core Ops, SparseCore 0:
  10.8 50.5 all-gather.2
  64.1 62.0 all-gather.4
  196.5 85.7 reduce-scatter.2
  286.5 69.0 reduce-scatter.4
